TPU v7x, 32 devices: a whole 2x2x4 slice. The times are simulated.
32 devices in a mesh: node: 4 (over y, x), space: 8 (over z, core).
Axes of the slice: x: 2, y: 2, z: 4, core: 2. Of those that a mesh axis runs over, the one named last changes fastest.
Arguments:
- snapshots: bfloat16 [512, 16, 8192], P('node', 'space'), may hold values from -8 to 8
- kappa: bfloat16 [16, 8192], P('space'), may hold values from 0.099609375 to 10
Outputs:
- gram: float32 [512, 512], P('node', 'space')
All inputs are finite; a program needn't handle non-finite values.
Results may differ from a plain program's by a relative error of at most 0.0003.
Values may be sent and summed in bfloat16 or wider, within the bound.
A program may use at most 128 MiB of HBM per device.

v0:
```python
import math

import jax
import jax.numpy as jnp
from jax import lax
from jax.sharding import PartitionSpec as P

NY = 128
NZ = 64


def extended(value, sides, width):
    for axis, dim in sides:
        size, length = (lax.axis_size(axis), value.shape[dim])
        up = [(i, (i + 1) % size) for i in range(size - 1)]
        down = [(j, i) for i, j in up]
        last = lax.slice_in_dim(value, length - width, length, axis=dim)
        first = lax.slice_in_dim(value, 0, width, axis=dim)
        before = lax.ppermute(last, axis, up)
        after = lax.ppermute(first, axis, down)
        value = jnp.concatenate([before, value, after], axis=dim)
    return value


def shifted(value, axis, by):
    length = lax.axis_size(axis)
    return lax.ppermute(value, axis, [(i, (i + by) % length) for i in range(length)])


def ahead(values, offset):
    tail = jnp.zeros(values.shape[:-1] + (offset,), values.dtype)
    return jnp.concatenate([values[..., offset:], tail], axis=-1)


def behind(values, offset):
    head = jnp.zeros(values.shape[:-1] + (offset,), values.dtype)
    return jnp.concatenate([head, values[..., :-offset]], axis=-1)


def flat_terms(field, kap_mid):
    width = field.shape[-1]
    zpos = jnp.arange(width, dtype=jnp.int32) % NZ
    up_ok = zpos != NZ - 1
    down_ok = zpos != 0
    near = jnp.where(up_ok, ahead(field, 1), 0.0)
    near_k = jnp.where(up_ok, ahead(kap_mid, 1), 0.0)
    total = 0.5 * (kap_mid + near_k) * (field - near)
    near = jnp.where(down_ok, behind(field, 1), 0.0)
    near_k = jnp.where(down_ok, behind(kap_mid, 1), 0.0)
    total = total + 0.5 * (kap_mid + near_k) * (field - near)
    total = total + 0.5 * (kap_mid + ahead(kap_mid, NZ)) * (field - ahead(field, NZ))
    total = total + 0.5 * (kap_mid + behind(kap_mid, NZ)) * (field - behind(field, NZ))
    return total


def per_device(snapshots, kappa):
    snap_rows, planes, width = snapshots.shape
    stacked = jnp.concatenate([snapshots, kappa[None]], axis=0)
    padded = extended(stacked, (("space", 1),), 1)
    field = padded[:snap_rows, 1:-1].astype(jnp.float32)
    kap_all = padded[snap_rows].astype(jnp.float32)
    kap_mid = kap_all[1:-1]
    total = flat_terms(field, kap_mid)
    total = total + 0.5 * (kap_mid + kap_all[:-2]) * (
        field - padded[:snap_rows, :-2].astype(jnp.float32)
    )
    total = total + 0.5 * (kap_mid + kap_all[2:]) * (
        field - padded[:snap_rows, 2:].astype(jnp.float32)
    )
    image = total.astype(jnp.bfloat16).reshape(snap_rows, planes * width)
    owned = snapshots.reshape(snap_rows, planes * width)
    scale = jnp.float32(1.0 / math.sqrt(planes * lax.axis_size("space") * NY * NZ))
    nodes = lax.axis_size("node")
    where_am = lax.axis_index("node")

    def place(carry_total, block, turn):
        source = (where_am - turn) % nodes
        tile = jnp.einsum("ic,jc->ij", image, block, preferred_element_type=jnp.float32)
        return lax.dynamic_update_slice(carry_total, tile, (jnp.int32(0), source * snap_rows))

    def advance(turn, carry):
        partial_rows, block = carry
        partial_rows = place(partial_rows, block, turn)
        block = shifted(block, "node", 1)
        return (partial_rows, block)

    start = jnp.zeros((snap_rows, nodes * snap_rows), jnp.float32)
    partial_rows, block = lax.fori_loop(0, nodes - 1, advance, (start, owned))
    partial_rows = place(partial_rows, block, nodes - 1)
    gram = lax.psum_scatter(partial_rows, "space", scatter_dimension=1, tiled=True)
    return gram * scale


def solution(mesh):
    placed = (P("node", "space", None), P("space", None))
    return jax.shard_map(
        per_device, mesh=mesh, in_specs=placed, out_specs=P("node", "space"), check_vma=False
    )
```

profile of v0, /device:TPU:0, one launch (start us, length us, event | category | flops | bytes accessed | tf_op | source)
XLA Modules:
  0.0 515.2 jit_solution(1764555314349376646)
XLA Ops:
  6.5 12.0 %slice_maximum_fusion = (bf16[129,1,8192]{2,1,0:T(2,128)(2,1)S(1)}, bf16[129,1,8192]{2,1,0:T(2,128)(2,1)S(1)}) fusion(bf16[1,2,8192]{2,1,0:T(2,128)(2,1)} %bitcast.44, bf16[128,2,8192]{2,1,0:T(2,128)(2,1)} %param.4), kind=kLoop, calls=%fused_computation.20 | loop fusion | flops 8454144 | bytes 8454144 | tf_op jit(solution)/shard_map/concatenate | solution.py:58
  18.6 2.3 copy.11
  20.9 4.0 collective-permute-start.1
  24.9 3.7 copy.12
  28.6 1.3 collective-permute-start.2
  29.9 9.6 %fusion.22 = (f32[128,2,8191]{2,1,0:T(2,128)}, f32[128,2,8191]{2,1,0:T(2,128)}) fusion(bf16[128,2,8192]{2,1,0:T(2,128)(2,1)S(1)} %copy-done), kind=kLoop, calls=%fused_computation.49 | loop fusion | bytes 33550336 | tf_op jit(solution)/shard_map/slice | solution.py:32
  39.5 6.8 %copy.32 = bf16[16,8,2,8192]{3,1,2,0:T(8,128)(2,1)} copy(bf16[16,8,2,8192]{3,2,1,0:T(2,128)(2,1)} %bitcast.39) | data formatting | bytes 8388608
  46.3 11.9 %fusion.23 = (f32[128,2,8128]{2,1,0:T(2,128)}, f32[128,2,8128]{2,1,0:T(2,128)}) fusion(bf16[128,2,8192]{2,1,0:T(2,128)(2,1)} %param.4), kind=kLoop, calls=%fused_computation.50 | loop fusion | bytes 33292288 | tf_op jit(solution)/shard_map/slice | solution.py:32
  58.2 6.4 %copy.13 = bf16[129,1,8192]{2,1,0:T(2,128)(2,1)S(1)} copy(bf16[129,1,8192]{2,0,1:T(8,128)(2,1)} %collective-permute-done.1) | data formatting | bytes 4227072 | tf_op jit(solution)/shard_map/ppermute | solution.py:19
  64.7 8.6 %copy.14 = bf16[129,1,8192]{2,1,0:T(2,128)(2,1)} copy(bf16[129,1,8192]{2,0,1:T(8,128)(2,1)} %collective-permute-done.2) | data formatting | bytes 4227072 | tf_op jit(solution)/shard_map/ppermute | solution.py:20
  73.3 1.0 fusion.16
  74.8 0.7 copy-done.2
  75.5 83.4 %fusion.11 = bf16[128,2,8192]{2,1,0:T(2,128)(2,1)} fusion(f32[128,2,8128]{2,1,0:T(2,128)} %get-tuple-element.161, f32[128,2,8128]{2,1,0:T(2,128)} %get-tuple-element.160, f32[128,2,8191]{2,1,0:T(2,128)} %get-tuple-element.159, pred[8192]{0:T(1024)(128)(4,1)S(1)} %get-tuple-element.172, f32[128,2,8191]{2,1,0:T(2,128)} %get-tuple-element.158, ...), kind=kLoop, calls=%fused_computation.18 | loop fusion | flops 69206016 | bytes 46479360 | tf_op jit(solution)/shard_map/convert_element_type | solution.py:70
  158.8 11.2 %copy.17 = bf16[128,2,8192]{0,2,1:T(8,128)(2,1)} copy(bf16[128,2,8192]{2,1,0:T(2,128)(2,1)} %fusion.11) | data formatting | bytes 8388608 | tf_op jit(solution)/shard_map/convert_element_type | solution.py:70
  170.0 6.5 %copy.18 = bf16[128,16384]{1,0:T(8,128)(2,1)} copy(bf16[128,16384]{0,1:T(8,128)(2,1)} %bitcast.40) | data formatting | bytes 8388608 | tf_op jit(solution)/shard_map/while | solution.py:88
  176.5 295.2 %while.17 = (s32[]{:T(128)}, f32[128,512]{0,1:T(8,128)S(1)}, bf16[128,16384]{1,0:T(8,128)(2,1)}, bf16[128,16384]{1,0:T(8,128)(2,1)}, s32[]{:T(128)}, /*index=5*/...) while((s32[]{:T(128)}, f32[128,512]{0,1:T(8,128)S(1)}, ...), condition=%wide.region_1.2_spmd, body=%wide.region_0.1_spmd.sunk | while | flops 536870912 | bytes 33620288 | solution.py:88
  176.5 4.5 copy.39
  181.0 2.3 collective-permute-start
  183.3 4.7 convolution_dynamic-update-slice_fusion.3
  188.0 87.4 %collective-permute-done = bf16[128,16384]{1,0:T(8,128)(2,1)} collective-permute-done((bf16[128,16384]{1,0:T(8,128)(2,1)}, bf16[128,16384]{1,0:T(8,128)(2,1)}, u32[]{:S(2)}, u32[]{:S(2)}) %collective-permute-start) | collective-permute-done | bytes 4194336 | tf_op jit(solution)/shard_map/while/body/eval_jaxpr/ppermute | solution.py:27
  275.5 4.5 copy.39
  280.0 1.5 collective-permute-start
  281.4 4.7 convolution_dynamic-update-slice_fusion.3
  286.1 87.9 %collective-permute-done = bf16[128,16384]{1,0:T(8,128)(2,1)} collective-permute-done((bf16[128,16384]{1,0:T(8,128)(2,1)}, bf16[128,16384]{1,0:T(8,128)(2,1)}, u32[]{:S(2)}, u32[]{:S(2)}) %collective-permute-start) | collective-permute-done | bytes 4194336 | tf_op jit(solution)/shard_map/while/body/eval_jaxpr/ppermute | solution.py:27
  374.0 4.5 copy.39
  378.5 0.3 collective-permute-start
  378.8 4.7 convolution_dynamic-update-slice_fusion.3
  383.5 88.2 %collective-permute-done = bf16[128,16384]{1,0:T(8,128)(2,1)} collective-permute-done((bf16[128,16384]{1,0:T(8,128)(2,1)}, bf16[128,16384]{1,0:T(8,128)(2,1)}, u32[]{:S(2)}, u32[]{:S(2)}) %collective-permute-start) | collective-permute-done | bytes 4194336 | tf_op jit(solution)/shard_map/while/body/eval_jaxpr/ppermute | solution.py:27
  471.7 4.7 convolution_dynamic-update-slice_fusion.1
  476.5 0.7 copy-done.3
  477.2 29.8 %reduce-scatter.2.cloned.1.call-done = f32[128,64]{0,1:T(8,128)} async-done(((f32[128,512]{0,1:T(8,128)}), f32[128,64]{0,1:T(8,128)}) %reduce-scatter.2.cloned.1.call-update) | async-done | bytes 32784 | tf_op jit(solution)/shard_map/reduce_scatter | solution.py:90
  507.0 1.4 broadcast_multiply_fusion
  (17 shorter events, 0.6 us)
Async XLA Ops:
  6.5 500.5 %reduce-scatter.2.cloned.1.call-start = ((), (), s32[]{:S(2)}) async-start(), calls=%async_computation.1 | async-start | bytes 294912 | tf_op jit(solution)/shard_map/reduce_scatter | solution.py:90
  20.9 9.1 %copy-start = (bf16[128,2,8192]{2,1,0:T(2,128)(2,1)S(1)}, bf16[128,2,8192]{2,1,0:T(2,128)(2,1)}, u32[]{:S(2)}) copy-start(bf16[128,2,8192]{2,1,0:T(2,128)(2,1)} %param.4) | copy-start | bytes 12582916
  20.9 37.4 %collective-permute-start.1 = (bf16[129,1,8192]{2,0,1:T(8,128)(2,1)S(1)}, bf16[129,1,8192]{2,0,1:T(8,128)(2,1)}, u32[]{:S(2)}, u32[]{:S(2)}) collective-permute-start(bf16[129,1,8192]{2,0,1:T(8,128)(2,1)S(1)} %copy.11), channel_id=1, source_target_pairs={{0,1},{1,2},{2,3},{3,4},{4,5},{5,6},{6,7},{8,9},{9,10},{10,11},{11... | collective-permute-start | bytes 6340616 | tf_op jit(solution)/shard_map/ppermute | solution.py:19
  28.6 36.1 %collective-permute-start.2 = (bf16[129,1,8192]{2,0,1:T(8,128)(2,1)}, bf16[129,1,8192]{2,0,1:T(8,128)(2,1)}, u32[]{:S(2)}, u32[]{:S(2)}) collective-permute-start(bf16[129,1,8192]{2,0,1:T(8,128)(2,1)} %copy.12), channel_id=1, source_target_pairs={{1,0},{2,1},{3,2},{4,3},{5,4},{6,5},{7,6},{9,8},{10,9},{11,10},{12... | collective-permute-start | bytes 6340616 | tf_op jit(solution)/shard_map/ppermute | solution.py:20
  64.7 8.6 %copy-start.1 = (bf16[128,2,8192]{2,1,0:T(2,128)(2,1)S(1)}, bf16[128,2,8192]{2,1,0:T(2,128)(2,1)}, u32[]{:S(2)}) copy-start(bf16[128,2,8192]{2,1,0:T(2,128)(2,1)} %param.4) | copy-start | bytes 12582916
  64.7 8.6 %copy-start.4 = (bf16[2,8192]{1,0:T(2,128)(2,1)S(1)}, bf16[2,8192]{1,0:T(2,128)(2,1)}, u32[]{:S(2)}) copy-start(bf16[2,8192]{1,0:T(2,128)(2,1)} %param.5) | copy-start | bytes 98308
  73.3 2.2 copy-start.2
  181.0 94.5 %collective-permute-start = (bf16[128,16384]{1,0:T(8,128)(2,1)}, bf16[128,16384]{1,0:T(8,128)(2,1)}, u32[]{:S(2)}, u32[]{:S(2)}) collective-permute-start(bf16[128,16384]{1,0:T(8,128)(2,1)} %copy.39), channel_id=1, source_target_pairs={{0,8},{8,16},{16,24},{24,0},{1,9},{9,17},{17,25},{25,1},{2,10},{10... | collective-permute-start | bytes 12582920 | tf_op jit(solution)/shard_map/while/body/eval_jaxpr/ppermute | solution.py:27
  280.0 94.1 %collective-permute-start = (bf16[128,16384]{1,0:T(8,128)(2,1)}, bf16[128,16384]{1,0:T(8,128)(2,1)}, u32[]{:S(2)}, u32[]{:S(2)}) collective-permute-start(bf16[128,16384]{1,0:T(8,128)(2,1)} %copy.39), channel_id=1, source_target_pairs={{0,8},{8,16},{16,24},{24,0},{1,9},{9,17},{17,25},{25,1},{2,10},{10... | collective-permute-start | bytes 12582920 | tf_op jit(solution)/shard_map/while/body/eval_jaxpr/ppermute | solution.py:27
  378.5 93.2 %collective-permute-start = (bf16[128,16384]{1,0:T(8,128)(2,1)}, bf16[128,16384]{1,0:T(8,128)(2,1)}, u32[]{:S(2)}, u32[]{:S(2)}) collective-permute-start(bf16[128,16384]{1,0:T(8,128)(2,1)} %copy.39), channel_id=1, source_target_pairs={{0,8},{8,16},{16,24},{24,0},{1,9},{9,17},{17,25},{25,1},{2,10},{10... | collective-permute-start | bytes 12582920 | tf_op jit(solution)/shard_map/while/body/eval_jaxpr/ppermute | solution.py:27
  476.5 0.7 copy-start.3
Sparse Core Ops, SparseCore 0:
  477.3 29.6 reduce-scatter.1
where the time goes:
time: 516 us; the launch traced here: 515 us
  waiting for transfers between devices  293 us (57%)
  other arithmetic  98 us (19%)
  local copies, waits for them, and re-layouts  82 us (16%)
  matrix products  18.8 us (4%)
  between operations  13.5 us (3%)
  starting transfers between devices  9.39 us (2%)
    ppermute x3, waiting for transfers between devices, shifted(): lax.ppermute(value, axis, [(i, (i + by) % length) for i in range(length)])  264 us
    convert_element_type x1, other arithmetic, per_device(): image = total.astype(jnp.bfloat16).reshape(snap_rows, planes * width)  83.4 us
    reduce_scatter x1, waiting for transfers between devices, per_device(): lax.psum_scatter(partial_rows, 'space', scatter_dimension=1, tiled=True)  29.8 us
    slice x4, local copies, waits for them, and re-layouts, ahead(): return jnp.concatenate([values[..., offset:], tail], axis=-1)  21.8 us
    dynamic_update_slice x3, matrix products, place(): lax.dynamic_update_slice(carry_total, tile, (jnp.int32(0), source * snap_...  14.1 us
    another operation x3, local copies, waits for them, and re-layouts  13.5 us
    concatenate x1, other arithmetic, per_device(): stacked = jnp.concatenate([snapshots, kappa[None]], axis=0)  12 us
    convert_element_type x1, local copies, waits for them, and re-layouts, per_device(): image = total.astype(jnp.bfloat16).reshape(snap_rows, planes * width)  11.2 us
  transfers between devices with their start and end apart: 6, of which 4 were waited for; matrix products, arithmetic and copies ran while one was open for 10% of the time, Pallas kernels for 0%

commit v1 on v0

v1 whole, which is shorter than its diff:
```python
import functools
import math

import jax
import jax.numpy as jnp
from jax import lax
from jax.experimental import pallas as pl
from jax.experimental.pallas import tpu as pltpu
from jax.sharding import PartitionSpec as P

NY = 128
NZ = 64
LANE = 128
ROWS = 16
MESH = pl.DeviceIdType.MESH


def packed(values, nodes):
    length = values.shape[-1] // nodes
    main = values.reshape(values.shape[:-1] + (nodes, length))
    none = jnp.zeros(main.shape[:-2] + (1, NZ), values.dtype)
    before = jnp.concatenate([none, main[..., :-1, -NZ:]], axis=-2)
    after = jnp.concatenate([main[..., 1:, :NZ], none], axis=-2)
    return jnp.concatenate([main, before, after], axis=-1)


def gram_kernel(
    nodes, spaces, xs_ref, kap_ref, out_ref,
    held, side, kside, coef, image,
    own_sem, send_sem, recv_sem, hsend, hrecv, ksend, krecv,
):
    me = lax.axis_index("node")
    at = lax.axis_index("space")
    snap_rows = xs_ref.shape[1]
    full = xs_ref.shape[2] // 2
    length = full - LANE
    tiles = length // LANE
    chunks = snap_rows // ROWS
    has_low = at > 0
    has_high = at < spaces - 1

    barrier = pltpu.get_barrier_semaphore()
    for turn in range(1, nodes):
        pl.semaphore_signal(
            barrier, inc=1, device_id={"node": lax.rem(me + turn, nodes)}, device_id_type=MESH
        )

    @pl.when(has_low)
    def _():
        pl.semaphore_signal(barrier, inc=1, device_id={"space": at - 1}, device_id_type=MESH)

    @pl.when(has_high)
    def _():
        pl.semaphore_signal(barrier, inc=1, device_id={"space": at + 1}, device_id_type=MESH)

    @pl.when(jnp.logical_not(has_low))
    def _():
        side[0] = jnp.zeros(side.shape[1:], side.dtype)
        kside[0] = jnp.zeros(kside.shape[1:], kside.dtype)

    @pl.when(jnp.logical_not(has_high))
    def _():
        side[1] = jnp.zeros(side.shape[1:], side.dtype)
        kside[1] = jnp.zeros(kside.shape[1:], kside.dtype)

    both = jnp.logical_and(has_low, has_high)

    @pl.when(both)
    def _():
        pl.semaphore_wait(barrier, nodes + 1)

    @pl.when(jnp.logical_not(both))
    def _():
        pl.semaphore_wait(barrier, nodes)

    def own_copy(chunk):
        rows = pl.ds(chunk * ROWS, ROWS)
        return pltpu.make_async_copy(
            xs_ref.at[me, rows], held.at[me, rows], own_sem.at[chunk]
        )

    def block_copy(chunk, turn):
        rows = pl.ds(chunk * ROWS, ROWS)
        peer = lax.rem(me + turn, nodes)
        return pltpu.make_async_remote_copy(
            src_ref=xs_ref.at[peer, rows],
            dst_ref=held.at[me, rows],
            send_sem=send_sem.at[turn - 1, chunk],
            recv_sem=recv_sem.at[turn - 1, chunk],
            device_id={"node": peer},
            device_id_type=MESH,
        )

    def side_copy(chunk, high):
        rows = pl.ds(chunk * ROWS, ROWS)
        return pltpu.make_async_remote_copy(
            src_ref=held.at[:, rows, pl.ds(full if high else 0, length)],
            dst_ref=side.at[0 if high else 1, :, rows],
            send_sem=hsend.at[0 if high else 1, chunk],
            recv_sem=hrecv.at[0 if high else 1, chunk],
            device_id={"space": at + 1 if high else at - 1},
            device_id_type=MESH,
        )

    def kappa_copy(high):
        return pltpu.make_async_remote_copy(
            src_ref=kap_ref.at[1 if high else 0],
            dst_ref=kside.at[0 if high else 1],
            send_sem=ksend.at[0 if high else 1],
            recv_sem=krecv.at[0 if high else 1],
            device_id={"space": at + 1 if high else at - 1},
            device_id_type=MESH,
        )

    @pl.when(has_high)
    def _():
        kappa_copy(True).start()

    @pl.when(has_low)
    def _():
        kappa_copy(False).start()

    def begin(chunk, carry):
        own_copy(chunk).start()
        for turn in range(1, nodes):
            block_copy(chunk, turn).start()
        return carry

    lax.fori_loop(0, chunks, begin, 0)

    @pl.when(has_high)
    def _():
        kappa_copy(True).wait_send()
        kappa_copy(False).wait_recv()

    @pl.when(has_low)
    def _():
        kappa_copy(False).wait_send()
        kappa_copy(True).wait_recv()

    lane = lax.broadcasted_iota(jnp.int32, (8, LANE), 1)
    lower = lane < NZ
    zpos = lane % NZ
    inner = jnp.where(zpos == NZ - 1, 0.0, 0.5).astype(jnp.float32)
    edge = jnp.where(zpos == 0, 0.5, jnp.where(zpos == NZ - 1, 0.5, 0.0)).astype(jnp.float32)

    def cols(tile, plane=0):
        return pl.ds(plane * full + tile * LANE, LANE)

    for plane in range(2):
        kap = [kap_ref[plane, :, cols(t)] for t in range(tiles + 1)]
        turned = [pltpu.roll(k, NZ, 1) for k in kap[:tiles]]
        for t in range(tiles):
            k = kap[t]
            up = jnp.where(lower, turned[t], turned[t + 1] if t + 1 < tiles else kap[tiles])
            down = jnp.where(lower, turned[t - 1] if t else kap[tiles], turned[t])
            coef[4 * plane, :, cols(t)] = inner * (k + pltpu.roll(k, LANE - 1, 1))
            coef[4 * plane + 1, :, cols(t)] = 0.5 * (k + up)
            coef[4 * plane + 2, :, cols(t)] = 0.5 * (k + down)
            coef[4 * plane + 3, :, cols(t)] = edge * k
    for t in range(tiles):
        low, high = (kap_ref[0, :, cols(t)], kap_ref[1, :, cols(t)])
        coef[8, :, cols(t)] = 0.5 * (low + kside[0, :, cols(t)])
        coef[9, :, cols(t)] = 0.5 * (low + high)
        coef[10, :, cols(t)] = 0.5 * (high + kside[1, :, cols(t)])

    def arrive(chunk):
        own_copy(chunk).wait()
        for turn in range(1, nodes):
            block_copy(chunk, turn).wait_recv()

        @pl.when(has_high)
        def _():
            side_copy(chunk, True).start()

        @pl.when(has_low)
        def _():
            side_copy(chunk, False).start()

    lower3 = lax.broadcasted_iota(jnp.int32, (ROWS // 8, 8, LANE), 2) < NZ

    def apply(chunk):
        @pl.when(has_high)
        def _():
            side_copy(chunk, False).wait_recv()

        @pl.when(has_low)
        def _():
            side_copy(chunk, True).wait_recv()

        rows = pl.ds(chunk * ROWS, ROWS)

        def one(node, carry):
            def wide(value):
                return value.astype(jnp.float32).reshape(ROWS // 8, 8, LANE)

            def load(plane, tile):
                return wide(held[node, rows, cols(tile, plane)])

            sides = [load(plane, tiles) for plane in range(2)]
            now = [load(plane, 0) for plane in range(2)]
            turned = [pltpu.roll(v, NZ, 2) for v in now]
            last = list(sides)
            for t in range(tiles):
                if t + 1 < tiles:
                    later = [load(plane, t + 1) for plane in range(2)]
                    coming = [pltpu.roll(v, NZ, 2) for v in later]
                else:
                    later, coming = (None, list(sides))
                mid = coef[9, :, cols(t)] * (now[0] - now[1])
                beside = [wide(side[p, node, rows, cols(t)]) for p in range(2)]
                for plane in range(2):
                    v = now[plane]
                    up = jnp.where(lower3, turned[plane], coming[plane])
                    down = jnp.where(lower3, last[plane], turned[plane])
                    flux = coef[4 * plane, :, cols(t)] * (v - pltpu.roll(v, LANE - 1, 2))
                    total = flux - pltpu.roll(flux, 1, 2)
                    total = total + coef[4 * plane + 3, :, cols(t)] * v
                    total = total + coef[4 * plane + 1, :, cols(t)] * (v - up)
                    total = total + coef[4 * plane + 2, :, cols(t)] * (v - down)
                    total = total + coef[8 + 2 * plane, :, cols(t)] * (v - beside[plane])
                    total = total - mid if plane else total + mid
                    image[node, rows, cols(t, plane)] = total.reshape(ROWS, LANE).astype(
                        jnp.bfloat16
                    )
                last, turned, now = (turned, coming, later)
            for plane in range(2):
                image[node, rows, cols(tiles, plane)] = jnp.zeros((ROWS, LANE), jnp.bfloat16)
            return carry

        lax.fori_loop(0, nodes, one, 0)

    arrive(0)

    def step(chunk, carry):
        arrive(chunk)
        apply(chunk - 1)
        return carry

    lax.fori_loop(1, chunks, step, 0)
    apply(chunks - 1)

    def product(index, carry):
        block, half = (index // 2, index % 2)
        left = image[pl.ds(block, 1)].reshape(snap_rows, 2 * full)
        right = held[pl.ds(half * 2, 2)].reshape(2 * snap_rows, 2 * full)
        tile = lax.dot_general(
            left, right, (((1,), (1,)), ((), ())), preferred_element_type=jnp.float32
        )
        out_ref[
            pl.ds(pl.multiple_of(block * snap_rows, snap_rows), snap_rows),
            pl.ds(pl.multiple_of(half * 2 * snap_rows, 2 * snap_rows), 2 * snap_rows),
        ] = tile
        return carry

    lax.fori_loop(0, 2 * nodes, product, 0)

    def finish(chunk, carry):
        for turn in range(1, nodes):
            block_copy(chunk, turn).wait_send()

        @pl.when(has_high)
        def _():
            side_copy(chunk, True).wait_send()

        @pl.when(has_low)
        def _():
            side_copy(chunk, False).wait_send()

        return carry

    lax.fori_loop(0, chunks, finish, 0)


def per_device(snapshots, kappa):


    snap_rows, planes, width = snapshots.shape
    nodes, spaces = (lax.axis_size("node"), lax.axis_size("space"))
    length = width // nodes
    full = length + LANE
    chunks = snap_rows // ROWS
    xs = packed(snapshots, nodes)
    xs = jnp.transpose(xs, (2, 0, 1, 3)).reshape(nodes, snap_rows, planes * full)
    kap = packed(kappa.astype(jnp.float32), nodes)
    kap = lax.dynamic_index_in_dim(kap, lax.axis_index("node"), axis=1, keepdims=True)
    kap = jnp.broadcast_to(kap, (planes, 8, full))
    order = nodes * snap_rows
    partial_rows = pl.pallas_call(
        functools.partial(gram_kernel, nodes, spaces),
        out_shape=jax.ShapeDtypeStruct((order, order), jnp.float32),
        in_specs=[
            pl.BlockSpec(memory_space=pl.ANY),
            pl.BlockSpec(memory_space=pltpu.VMEM),
        ],
        out_specs=pl.BlockSpec(memory_space=pltpu.VMEM),
        scratch_shapes=[
            pltpu.VMEM((nodes, snap_rows, planes * full), jnp.bfloat16),
            pltpu.VMEM((2, nodes, snap_rows, length), jnp.bfloat16),
            pltpu.VMEM((2, 8, full), jnp.float32),
            pltpu.VMEM((11, 8, length), jnp.float32),
            pltpu.VMEM((nodes, snap_rows, planes * full), jnp.bfloat16),
            pltpu.SemaphoreType.DMA((chunks,)),
            pltpu.SemaphoreType.DMA((nodes - 1, chunks)),
            pltpu.SemaphoreType.DMA((nodes - 1, chunks)),
            pltpu.SemaphoreType.DMA((2, chunks)),
            pltpu.SemaphoreType.DMA((2, chunks)),
            pltpu.SemaphoreType.DMA((2,)),
            pltpu.SemaphoreType.DMA((2,)),
        ],
        compiler_params=pltpu.CompilerParams(
            collective_id=0, has_side_effects=True, vmem_limit_bytes=40 * 1024 * 1024
        ),
        name="gram_parts",
    )(xs, kap)
    mine = lax.psum_scatter(partial_rows, "node", scatter_dimension=0, tiled=True)
    gram = lax.psum_scatter(mine, "space", scatter_dimension=1, tiled=True)
    return gram * jnp.float32(1.0 / math.sqrt(planes * spaces * NY * NZ))


def solution(mesh):
    placed = (P("node", "space", None), P("space", None))
    return jax.shard_map(
        per_device, mesh=mesh, in_specs=placed, out_specs=P("node", "space"), check_vma=False
    )
```

time: 516 us -> 187 us (0.36)
  waiting for transfers between devices: 293 us -> 62.1 us
  other arithmetic: 98 us -> 1.38 us
  Pallas kernels: 0 us -> 65.1 us
  local copies, waits for them, and re-layouts: 82 us -> 43.8 us
  matrix products: 18.8 us -> 0 us
  starting transfers between devices: 9.39 us -> 0.04 us
    ppermute x5 -> x0, waiting for transfers between devices: 264 us -> none  [the longest x3 264 us: shifted(): lax.ppermute(value, axis, [(i, (i + by) % length) for i in range(length)])]
    convert_element_type x2 -> x0, other arithmetic: 84.4 us -> none  [the longest x1 83.4 us: per_device(): image = total.astype(jnp.bfloat16).reshape(snap_rows, planes * width)]
    pallas_call x0 -> x1, Pallas kernels: none -> 65.1 us  [per_device(): pl.pallas_call(functools.partial(gram_kernel, nodes, spaces), out_shape=j...]
    unnamed x1 -> x3, waiting for transfers between devices: 0.02 us -> 30.9 us
    slice x6 -> x2, local copies, waits for them, and re-layouts: 27.8 us -> 0.44 us  [packed(): after = jnp.concatenate([main[..., 1:, :NZ], none], axis=-2)]
    concatenate x0 -> x6, local copies, waits for them, and re-layouts: none -> 24.2 us  [the longest x2 23.7 us: packed(): return jnp.concatenate([main, before, after], axis=-1)]
    ppermute x2 -> x0, local copies, waits for them, and re-layouts: 15 us -> none  [the longest x1 8.56 us: extended(): after = lax.ppermute(first, axis, down)]
    dynamic_update_slice x3 -> x0, matrix products: 14.1 us -> none  [place(): lax.dynamic_update_slice(carry_total, tile, (jnp.int32(0), source * snap_...]
  transfers between devices with their start and end apart: 6 -> 2, of which waited for: 4 -> 2; matrix products, arithmetic and copies ran while one was open for 10% -> 0% of each run, Pallas kernels for 0% -> 0%
where the time goes in v1:
time: 187 us; the launch traced here: 186 us
  Pallas kernels  65.1 us (35%)
  waiting for transfers between devices  62.1 us (33%)
  local copies, waits for them, and re-layouts  43.8 us (23%)
  between operations  13.5 us (7%)
    pallas_call x1, Pallas kernels, per_device(): pl.pallas_call(functools.partial(gram_kernel, nodes, spaces), out_shape=j...  65.1 us
    reduce_scatter x1, waiting for transfers between devices, per_device(): lax.psum_scatter(partial_rows, 'node', scatter_dimension=0, tiled=True)  31.2 us
    unnamed x3, waiting for transfers between devices  30.9 us
    concatenate x2, local copies, waits for them, and re-layouts, packed(): return jnp.concatenate([main, before, after], axis=-1)  23.7 us
    reshape x1, local copies, waits for them, and re-layouts, per_device(): jnp.transpose(xs, (2, 0, 1, 3)).reshape(nodes, snap_rows, planes * full)  7.83 us
    unnamed x8, local copies, waits for them, and re-layouts  6.04 us
    reshape x2, local copies, waits for them, and re-layouts, packed(): main = values.reshape(values.shape[:-1] + (nodes, length))  5.35 us
  transfers between devices with their start and end apart: 2, of which 2 were waited for; matrix products, arithmetic and copies ran while one was open for 0% of the time, Pallas kernels for 0%

profile of v1, /device:TPU:0, one launch (start us, length us, event | category | flops | bytes accessed | tf_op | source)
XLA Modules:
  0.0 185.9 jit_solution(2002860841651725116)
XLA Ops:
  6.5 0.0 reduce-scatter.5.cloned.1.call-start
  6.5 5.3 %copy.21 = bf16[128,1,4,2,2048]{4,3,1,0,2:T(2,128)(2,1)S(1)} copy(bf16[128,1,4,2,2048]{4,3,2,1,0:T(2,128)(2,1)} %bitcast.14) | data formatting | bytes 8388608 | tf_op jit(solution)/shard_map/reshape | solution.py:20
  11.9 0.0 copy-start.1
  11.9 2.0 %copy-done.1 = bf16[128,1,4,2,2048]{4,3,1,0,2:T(2,128)(2,1)} copy-done((bf16[128,1,4,2,2048]{4,3,1,0,2:T(2,128)(2,1)}, bf16[128,1,4,2,2048]{4,3,1,0,2:T(2,128)(2,1)S(1)}, u32[]{:S(2)}) %copy-start.1) | copy-done | bytes 4194328
  13.9 0.4 fusion
  14.2 0.2 concatenate.18
  14.5 0.2 concatenate.19
  14.7 23.6 %concatenate.20 = bf16[128,2,4,2176]{3,1,0,2:T(2,128)(2,1)} concatenate(bf16[128,2,4,2048]{3,1,0,2:T(2,128)(2,1)} %bitcast.12, bf16[128,2,4,64]{3,1,0,2:T(2,128)(2,1)S(1)} %concatenate.18, bf16[128,2,4,64]{3,1,0,2:T(2,128)(2,1)S(1)} %concatenate.19), dimensions={3} | concatenate | bytes 8912896 | tf_op jit(solution)/shard_map/concatenate | solution.py:24
  38.3 0.0 copy-start.2
  38.3 7.8 %reshape.13.xs_ref = bf16[4,128,4352]{2,1,0:T(8,128)(2,1)} reshape(bf16[4,128,2,2176]{3,2,1,0:T(2,128)(2,1)} %bitcast.13) | data formatting | bytes 8912896 | tf_op jit(solution)/shard_map/reshape | solution.py:284
  46.1 0.0 copy-done.2
  46.2 0.1 fusion.1
  46.3 0.1 concatenate.23
  46.4 0.0 copy-start
  46.4 2.3 %copy-done = bf16[4,128,4352]{2,1,0:T(8,128)(2,1)S(1)} copy-done((bf16[4,128,4352]{2,1,0:T(8,128)(2,1)S(1)}, bf16[4,128,4352]{2,1,0:T(8,128)(2,1)}, u32[]{:S(2)}) %copy-start) | copy-done | bytes 4456472
  48.7 65.1 %gram_parts.1 = f32[512,512]{1,0:T(8,128)} custom-call(bf16[4,128,4352]{2,1,0:T(8,128)(2,1)S(1)} %copy-done, f32[2,8,2176]{2,1,0:T(8,128)S(1)} %broadcast_in_dim.10.kap_ref), custom_call_target="tpu_custom_call" | custom-call | tf_op jit(solution)/shard_map/gram_parts/pallas_call | solution.py:289
  113.8 0.0 reduce-scatter.5.cloned.1.call-update
  113.8 0.0 reduce-scatter.7.cloned.1.call-start
  113.8 31.2 %reduce-scatter.5.cloned.1.call-done = f32[128,512]{1,0:T(8,128)} async-done(((f32[512,512]{1,0:T(8,128)}), f32[128,512]{1,0:T(8,128)}) %reduce-scatter.5.cloned.1.call-update) | async-done | bytes 262160 | tf_op jit(solution)/shard_map/reduce_scatter | solution.py:316
  145.0 1.8 copy.15
  146.8 0.0 reduce-scatter.7.cloned.1.call-update
  146.8 30.9 %reduce-scatter.7.cloned.1.call-done = f32[64,128]{1,0:T(8,128)} async-done(((f32[512,128]{1,0:T(8,128)}), f32[64,128]{1,0:T(8,128)}) %reduce-scatter.7.cloned.1.call-update) | async-done | bytes 32784
  177.7 1.4 bitcast_multiply_fusion
  (6 shorter events, 0.1 us)
Async XLA Ops:
  6.5 138.5 %reduce-scatter.5.cloned.1.call-start = ((), (), s32[]{:S(2)}) async-start(), calls=%async_computation.2 | async-start | bytes 1310720 | tf_op jit(solution)/shard_map/reduce_scatter | solution.py:316
  11.9 2.0 %copy-start.1 = (bf16[128,1,4,2,2048]{4,3,1,0,2:T(2,128)(2,1)}, bf16[128,1,4,2,2048]{4,3,1,0,2:T(2,128)(2,1)S(1)}, u32[]{:S(2)}) copy-start(bf16[128,1,4,2,2048]{4,3,1,0,2:T(2,128)(2,1)S(1)} %copy.21) | copy-start | bytes 12582916
  38.3 7.8 %copy-start.2 = (bf16[2,8192]{1,0:T(2,128)(2,1)S(1)}, bf16[2,8192]{1,0:T(2,128)(2,1)}, u32[]{:S(2)}) copy-start(bf16[2,8192]{1,0:T(2,128)(2,1)} %param.3) | copy-start | bytes 98308
  46.4 2.3 %copy-start = (bf16[4,128,4352]{2,1,0:T(8,128)(2,1)S(1)}, bf16[4,128,4352]{2,1,0:T(8,128)(2,1)}, u32[]{:S(2)}) copy-start(bf16[4,128,4352]{2,1,0:T(8,128)(2,1)} %reshape.13.xs_ref) | copy-start | bytes 13369348
  113.8 63.9 %reduce-scatter.7.cloned.1.call-start = ((), (), s32[]{:S(2)}) async-start(), calls=%async_computation.3 | async-start | bytes 294912
Sparse Core Ops, SparseCore 0:
  113.9 31.0 reduce-scatter.4
  147.3 30.3 reduce-scatter.6

commit v2 on v1

v2 whole, which is shorter than its diff:
```python
import functools
import math

import jax
import jax.numpy as jnp
from jax import lax
from jax.experimental import pallas as pl
from jax.experimental.pallas import tpu as pltpu
from jax.sharding import PartitionSpec as P

NY = 128
NZ = 64
LANE = 128
ROWS = 16
MESH = pl.DeviceIdType.MESH


def gram_kernel(
    nodes, spaces, scale, snap_ref, kap_ref, out_ref,
    held, ends, ends_out, edge, side, kside, coef, image, gram, first, second, third, fourth,
    own_sem, edge_sem, send_sem, recv_sem, esend, erecv, hsend, hrecv, ksend, krecv,
    send1, recv1, send2, recv2, send3, recv3, send4, recv4,
):
    me = lax.axis_index("node")
    at = lax.axis_index("space")
    snap_rows = snap_ref.shape[1]
    length = snap_ref.shape[2] // nodes
    tiles = length // LANE
    chunks = snap_rows // ROWS
    has_low = at > 0
    has_high = at < spaces - 1
    summed = out_ref.shape[0] == snap_rows
    layers = spaces // 2 if summed else 1

    def edge_copy(index):
        return pltpu.make_async_copy(
            snap_ref.at[:, :, pl.ds((index + 1) * length - LANE, 2 * LANE)],
            edge.at[index],
            edge_sem.at[index],
        )

    for index in range(nodes - 1):
        edge_copy(index).start()

    barrier = pltpu.get_barrier_semaphore()
    for turn in range(1, nodes):
        pl.semaphore_signal(
            barrier, inc=1, device_id={"node": lax.rem(me + turn, nodes)}, device_id_type=MESH
        )
    for turn in range(1, layers):
        pl.semaphore_signal(
            barrier,
            inc=1,
            device_id={"space": lax.rem(at + 2 * turn, spaces)},
            device_id_type=MESH,
        )

    @pl.when(has_low)
    def _():
        pl.semaphore_signal(barrier, inc=1, device_id={"space": at - 1}, device_id_type=MESH)

    @pl.when(has_high)
    def _():
        pl.semaphore_signal(barrier, inc=1, device_id={"space": at + 1}, device_id_type=MESH)

    @pl.when(jnp.logical_not(has_low))
    def _():
        side[0] = jnp.zeros(side.shape[1:], side.dtype)
        kside[0] = jnp.zeros(kside.shape[1:], kside.dtype)

    @pl.when(jnp.logical_not(has_high))
    def _():
        side[1] = jnp.zeros(side.shape[1:], side.dtype)
        kside[1] = jnp.zeros(kside.shape[1:], kside.dtype)

    both = jnp.logical_and(has_low, has_high)

    @pl.when(both)
    def _():
        pl.semaphore_wait(barrier, nodes + layers)

    @pl.when(jnp.logical_not(both))
    def _():
        pl.semaphore_wait(barrier, nodes + layers - 1)

    def own_copy(chunk):
        rows = pl.ds(chunk * ROWS, ROWS)
        return pltpu.make_async_copy(
            snap_ref.at[:, rows, pl.ds(pl.multiple_of(me * length, LANE), length)],
            held.at[me, :, rows],
            own_sem.at[chunk],
        )

    def block_copy(chunk, turn):
        rows = pl.ds(chunk * ROWS, ROWS)
        peer = lax.rem(me + turn, nodes)
        return pltpu.make_async_remote_copy(
            src_ref=snap_ref.at[:, rows, pl.ds(pl.multiple_of(peer * length, LANE), length)],
            dst_ref=held.at[me, :, rows],
            send_sem=send_sem.at[turn - 1, chunk],
            recv_sem=recv_sem.at[turn - 1, chunk],
            device_id={"node": peer},
            device_id_type=MESH,
        )

    def side_copy(chunk, high):
        rows = pl.ds(chunk * ROWS, ROWS)
        return pltpu.make_async_remote_copy(
            src_ref=held.at[:, 1 if high else 0, rows],
            dst_ref=side.at[0 if high else 1, :, rows],
            send_sem=hsend.at[0 if high else 1, chunk],
            recv_sem=hrecv.at[0 if high else 1, chunk],
            device_id={"space": at + 1 if high else at - 1},
            device_id_type=MESH,
        )

    def kappa_copy(high):
        return pltpu.make_async_remote_copy(
            src_ref=kap_ref.at[1 if high else 0, :, pl.ds(pl.multiple_of(me * length, LANE), length)],
            dst_ref=kside.at[0 if high else 1],
            send_sem=ksend.at[0 if high else 1],
            recv_sem=krecv.at[0 if high else 1],
            device_id={"space": at + 1 if high else at - 1},
            device_id_type=MESH,
        )

    def ends_copy(turn):
        peer = lax.rem(me + turn, nodes)
        return pltpu.make_async_remote_copy(
            src_ref=ends_out.at[peer],
            dst_ref=ends.at[me],
            send_sem=esend.at[turn - 1],
            recv_sem=erecv.at[turn - 1],
            device_id={"node": peer},
            device_id_type=MESH,
        )

    @pl.when(has_high)
    def _():
        kappa_copy(True).start()

    @pl.when(has_low)
    def _():
        kappa_copy(False).start()

    def begin(chunk, carry):
        own_copy(chunk).start()
        for turn in range(1, nodes):
            block_copy(chunk, turn).start()
        return carry

    begin(0, 0)
    for index in range(nodes - 1):
        edge_copy(index).wait()

    wide_lower = lax.broadcasted_iota(jnp.int32, (snap_rows, LANE), 1) < NZ
    for dest in range(nodes):
        for plane in range(2):
            before = after = jnp.zeros((snap_rows, LANE), jnp.float32)
            if dest:
                before = pltpu.roll(edge[dest - 1, plane, :, :LANE].astype(jnp.float32), NZ, 1)
            if dest < nodes - 1:
                after = pltpu.roll(edge[dest, plane, :, LANE:].astype(jnp.float32), NZ, 1)
            ends_out[dest, plane] = jnp.where(wide_lower, before, after).astype(jnp.bfloat16)
    for turn in range(1, nodes):
        ends_copy(turn).start()
    ends[me] = ends_out[me]
    lax.fori_loop(1, chunks, begin, 0)

    @pl.when(has_high)
    def _():
        kappa_copy(True).wait_send()
        kappa_copy(False).wait_recv()

    @pl.when(has_low)
    def _():
        kappa_copy(False).wait_send()
        kappa_copy(True).wait_recv()

    lane = lax.broadcasted_iota(jnp.int32, (8, LANE), 1)
    lower = lane < NZ
    zpos = lane % NZ
    inner = jnp.where(zpos == NZ - 1, 0.0, 0.5).astype(jnp.float32)
    rim = jnp.where(zpos == 0, 0.5, jnp.where(zpos == NZ - 1, 0.5, 0.0)).astype(jnp.float32)

    def cols(tile):
        return pl.ds(tile * LANE, LANE)

    def mine(tile):
        return pl.ds(pl.multiple_of((me * tiles + tile) * LANE, LANE), LANE)

    low_at = pl.ds(pl.multiple_of(jnp.maximum(me * tiles - 1, 0) * LANE, LANE), LANE)
    high_at = pl.ds(
        pl.multiple_of(jnp.minimum((me + 1) * tiles, nodes * tiles - 1) * LANE, LANE), LANE
    )
    for plane in range(2):
        kap = [kap_ref[plane, :, mine(t)] for t in range(tiles)]
        turned = [pltpu.roll(k, NZ, 1) for k in kap]
        before = pltpu.roll(kap_ref[plane, :, low_at], NZ, 1)
        after = pltpu.roll(kap_ref[plane, :, high_at], NZ, 1)
        before = before * jnp.where(me > 0, 1.0, 0.0)
        after = after * jnp.where(me < nodes - 1, 1.0, 0.0)
        for t in range(tiles):
            k = kap[t]
            up = jnp.where(lower, turned[t], turned[t + 1] if t + 1 < tiles else after)
            down = jnp.where(lower, turned[t - 1] if t else before, turned[t])
            coef[4 * plane, :, cols(t)] = inner * (k + pltpu.roll(k, LANE - 1, 1))
            coef[4 * plane + 1, :, cols(t)] = 0.5 * (k + up)
            coef[4 * plane + 2, :, cols(t)] = 0.5 * (k + down)
            coef[4 * plane + 3, :, cols(t)] = rim * k
    for t in range(tiles):
        low, high = (kap_ref[0, :, mine(t)], kap_ref[1, :, mine(t)])
        coef[8, :, cols(t)] = 0.5 * (low + kside[0, :, cols(t)])
        coef[9, :, cols(t)] = 0.5 * (low + high)
        coef[10, :, cols(t)] = 0.5 * (high + kside[1, :, cols(t)])

    def arrive(chunk):
        own_copy(chunk).wait()
        for turn in range(1, nodes):
            block_copy(chunk, turn).wait_recv()

        @pl.when(has_high)
        def _():
            side_copy(chunk, True).start()

        @pl.when(has_low)
        def _():
            side_copy(chunk, False).start()

    lower3 = lax.broadcasted_iota(jnp.int32, (ROWS // 8, 8, LANE), 2) < NZ

    def apply(chunk):
        @pl.when(has_high)
        def _():
            side_copy(chunk, False).wait_recv()

        @pl.when(has_low)
        def _():
            side_copy(chunk, True).wait_recv()

        rows = pl.ds(chunk * ROWS, ROWS)

        def one(node, carry):
            def wide(value):
                return value.astype(jnp.float32).reshape(ROWS // 8, 8, LANE)

            def load(plane, tile):
                return wide(held[node, plane, rows, cols(tile)])

            sides = [wide(ends[node, plane, rows, :]) for plane in range(2)]
            now = [load(plane, 0) for plane in range(2)]
            turned = [pltpu.roll(v, NZ, 2) for v in now]
            last = list(sides)
            for t in range(tiles):
                if t + 1 < tiles:
                    later = [load(plane, t + 1) for plane in range(2)]
                    coming = [pltpu.roll(v, NZ, 2) for v in later]
                else:
                    later, coming = (None, list(sides))
                mid = coef[9, :, cols(t)] * (now[0] - now[1])
                beside = [wide(side[p, node, rows, cols(t)]) for p in range(2)]
                for plane in range(2):
                    v = now[plane]
                    up = jnp.where(lower3, turned[plane], coming[plane])
                    down = jnp.where(lower3, last[plane], turned[plane])
                    flux = coef[4 * plane, :, cols(t)] * (v - pltpu.roll(v, LANE - 1, 2))
                    total = flux - pltpu.roll(flux, 1, 2)
                    total = total + coef[4 * plane + 3, :, cols(t)] * v
                    total = total + coef[4 * plane + 1, :, cols(t)] * (v - up)
                    total = total + coef[4 * plane + 2, :, cols(t)] * (v - down)
                    total = total + coef[8 + 2 * plane, :, cols(t)] * (v - beside[plane])
                    total = total - mid if plane else total + mid
                    image[node, plane, rows, cols(t)] = total.reshape(ROWS, LANE).astype(
                        jnp.bfloat16
                    )
                last, turned, now = (turned, coming, later)
            return carry

        lax.fori_loop(0, nodes, one, 0)

    arrive(0)
    for turn in range(1, nodes):
        ends_copy(turn).wait_recv()

    def step(chunk, carry):
        arrive(chunk)
        apply(chunk - 1)
        return carry

    lax.fori_loop(1, chunks, step, 0)
    apply(chunks - 1)

    order = nodes * snap_rows
    half = snap_rows // 2
    core = lax.rem(at, 2)
    partner = at + 1 - 2 * core
    layer = at // 2
    kept = pl.ds(pl.multiple_of(core * half, half), half)
    given = pl.ds(pl.multiple_of((1 - core) * half, half), half)

    def product(block):
        def part(index, carry):
            tile = jnp.zeros((snap_rows, 2 * snap_rows), jnp.float32)
            for plane in range(2):
                right = held[pl.ds(index * 2, 2), plane].reshape(2 * snap_rows, length)
                tile = tile + lax.dot_general(
                    image[block, plane], right, (((1,), (1,)), ((), ())),
                    preferred_element_type=jnp.float32,
                )
            place = pl.ds(pl.multiple_of(index * 2 * snap_rows, 2 * snap_rows), 2 * snap_rows)
            gram[block, :, place] = tile
            return carry

        lax.fori_loop(0, nodes // 2, part, 0)

    def first_copy(turn):
        block = lax.rem(me + turn, nodes)
        return pltpu.make_async_remote_copy(
            src_ref=gram.at[block, given],
            dst_ref=first.at[turn],
            send_sem=send1.at[turn],
            recv_sem=recv1.at[turn],
            device_id={"space": partner},
            device_id_type=MESH,
        )

    def second_copy(turn):
        return pltpu.make_async_remote_copy(
            src_ref=first.at[turn],
            dst_ref=second.at[turn - 1],
            send_sem=send2.at[turn - 1],
            recv_sem=recv2.at[turn - 1],
            device_id={"node": lax.rem(me + turn, nodes)},
            device_id_type=MESH,
        )

    def third_copy(turn):
        dest = lax.rem(layer + turn, layers)
        return pltpu.make_async_remote_copy(
            src_ref=first.at[0, :, pl.ds(pl.multiple_of(dest * LANE, LANE), LANE)],
            dst_ref=third.at[turn - 1],
            send_sem=send3.at[turn - 1],
            recv_sem=recv3.at[turn - 1],
            device_id={"space": lax.rem(at + 2 * turn, spaces)},
            device_id_type=MESH,
        )

    fourth_copy = pltpu.make_async_remote_copy(
        src_ref=fourth.at[0],
        dst_ref=fourth.at[1],
        send_sem=send4,
        recv_sem=recv4,
        device_id={"space": partner},
        device_id_type=MESH,
    )

    turns = list(range(1, nodes)) + [0]

    def paired(turn):
        first_copy(turn).wait_recv()
        block = lax.rem(me + turn, nodes)
        first[turn] = first[turn] + gram[block, kept]
        if turn:
            second_copy(turn).start()

    if summed:
        for place, turn in enumerate(turns):
            product(lax.rem(me + turn, nodes))
            first_copy(turn).start()
            if place:
                paired(turns[place - 1])
        paired(0)
        for turn in range(1, nodes):
            second_copy(turn).wait_recv()
            first[0] = first[0] + second[turn - 1]
        for turn in range(1, layers):
            third_copy(turn).start()
        own = first[0, :, pl.ds(pl.multiple_of(layer * LANE, LANE), LANE)]
        for turn in range(1, layers):
            third_copy(turn).wait_recv()
            own = own + third[turn - 1]
        fourth[0] = own * scale
        fourth_copy.start()
        fourth_copy.wait()
        width = LANE // 2

        def taken(value):
            return jnp.where(core == 0, value[:, :width], value[:, width:])

        out_ref[kept] = taken(fourth[0])
        out_ref[given] = taken(fourth[1])
        for turn in range(nodes):
            first_copy(turn).wait_send()
        for turn in range(1, nodes):
            second_copy(turn).wait_send()
        for turn in range(1, layers):
            third_copy(turn).wait_send()
    else:
        for block in range(nodes):
            product(block)
            out_ref[block * snap_rows : (block + 1) * snap_rows] = gram[block]
    for turn in range(1, nodes):
        ends_copy(turn).wait_send()

    def finish(chunk, carry):
        for turn in range(1, nodes):
            block_copy(chunk, turn).wait_send()

        @pl.when(has_high)
        def _():
            side_copy(chunk, True).wait_send()

        @pl.when(has_low)
        def _():
            side_copy(chunk, False).wait_send()

        return carry

    lax.fori_loop(0, chunks, finish, 0)


def per_device(snapshots, kappa):
    snap_rows, planes, width = snapshots.shape
    nodes, spaces = (lax.axis_size("node"), lax.axis_size("space"))
    length = width // nodes
    chunks = snap_rows // ROWS
    order = nodes * snap_rows
    half = snap_rows // 2
    scale = 1.0 / math.sqrt(planes * spaces * NY * NZ)
    summed = order // spaces == LANE // 2
    layers = spaces // 2
    shape = (snap_rows, order // spaces) if summed else (order, order)
    result = pl.pallas_call(
        functools.partial(gram_kernel, nodes, spaces, scale),
        out_shape=jax.ShapeDtypeStruct(shape, jnp.float32),
        in_specs=[
            pl.BlockSpec(memory_space=pl.ANY),
            pl.BlockSpec(memory_space=pltpu.VMEM),
        ],
        out_specs=pl.BlockSpec(memory_space=pltpu.VMEM),
        scratch_shapes=[
            pltpu.VMEM((nodes, planes, snap_rows, length), jnp.bfloat16),
            pltpu.VMEM((nodes, planes, snap_rows, LANE), jnp.bfloat16),
            pltpu.VMEM((nodes, planes, snap_rows, LANE), jnp.bfloat16),
            pltpu.VMEM((nodes - 1, planes, snap_rows, 2 * LANE), jnp.bfloat16),
            pltpu.VMEM((2, nodes, snap_rows, length), jnp.bfloat16),
            pltpu.VMEM((2, 8, length), jnp.float32),
            pltpu.VMEM((11, 8, length), jnp.float32),
            pltpu.VMEM((nodes, planes, snap_rows, length), jnp.bfloat16),
            pltpu.VMEM((nodes, snap_rows, order), jnp.float32),
            pltpu.VMEM((nodes, half, order), jnp.float32),
            pltpu.VMEM((nodes - 1, half, order), jnp.float32),
            pltpu.VMEM((layers - 1, half, LANE), jnp.float32),
            pltpu.VMEM((2, half, LANE), jnp.float32),
            pltpu.SemaphoreType.DMA((chunks,)),
            pltpu.SemaphoreType.DMA((nodes - 1,)),
            pltpu.SemaphoreType.DMA((nodes - 1, chunks)),
            pltpu.SemaphoreType.DMA((nodes - 1, chunks)),
            pltpu.SemaphoreType.DMA((nodes - 1,)),
            pltpu.SemaphoreType.DMA((nodes - 1,)),
            pltpu.SemaphoreType.DMA((2, chunks)),
            pltpu.SemaphoreType.DMA((2, chunks)),
            pltpu.SemaphoreType.DMA((2,)),
            pltpu.SemaphoreType.DMA((2,)),
            pltpu.SemaphoreType.DMA((nodes,)),
            pltpu.SemaphoreType.DMA((nodes,)),
            pltpu.SemaphoreType.DMA((nodes - 1,)),
            pltpu.SemaphoreType.DMA((nodes - 1,)),
            pltpu.SemaphoreType.DMA((layers - 1,)),
            pltpu.SemaphoreType.DMA((layers - 1,)),
            pltpu.SemaphoreType.DMA,
            pltpu.SemaphoreType.DMA,
        ],
        compiler_params=pltpu.CompilerParams(
            collective_id=0, has_side_effects=True, vmem_limit_bytes=48 * 1024 * 1024
        ),
        name="gram_sums",
    )(
        jnp.transpose(snapshots, (1, 0, 2)),
        jnp.broadcast_to(kappa.astype(jnp.float32)[:, None], (planes, 8, width)),
    )
    if summed:
        return result
    mine = lax.psum_scatter(result, "node", scatter_dimension=0, tiled=True)
    return lax.psum_scatter(mine, "space", scatter_dimension=1, tiled=True) * scale


def solution(mesh):
    placed = (P("node", "space", None), P("space", None))
    return jax.shard_map(
        per_device, mesh=mesh, in_specs=placed, out_specs=P("node", "space"), check_vma=False
    )
```

time: 187 us -> 85.9 us (0.46)
  waiting for transfers between devices: 62.1 us -> 0 us
  local copies, waits for them, and re-layouts: 43.8 us -> 6.35 us
  Pallas kernels: 65.1 us -> 79.3 us
  between operations: 13.5 us -> 0.02 us
    reduce_scatter x1 -> x0, waiting for transfers between devices: 31.2 us -> none  [per_device(): lax.psum_scatter(partial_rows, 'node', scatter_dimension=0, tiled=True)]
    unnamed x3 -> x0, waiting for transfers between devices: 30.9 us -> none
    concatenate x6 -> x0, local copies, waits for them, and re-layouts: 24.2 us -> none  [the longest x2 23.7 us: packed(): return jnp.concatenate([main, before, after], axis=-1)]
    pallas_call x1, Pallas kernels: 65.1 us -> 79.3 us  [per_device(): pl.pallas_call(functools.partial(gram_kernel, nodes, spaces, scale), out_...]
    reshape x3 -> x0, local copies, waits for them, and re-layouts: 13.2 us -> none  [the longest x1 7.83 us: per_device(): jnp.transpose(xs, (2, 0, 1, 3)).reshape(nodes, snap_rows, planes * full)]
    unnamed x8 -> x1, local copies, waits for them, and re-layouts: 6.04 us -> 4.86 us
  transfers between devices with their start and end apart: 2 -> 0, of which waited for: 2 -> 0; matrix products, arithmetic and copies ran while one was open for 0% -> 0% of each run, Pallas kernels for 0% -> 0%
where the time goes in v2:
time: 85.9 us; the launch traced here: 85.7 us
  Pallas kernels  79.3 us (92%)
  local copies, waits for them, and re-layouts  6.35 us (7%)
    pallas_call x1, Pallas kernels, per_device(): pl.pallas_call(functools.partial(gram_kernel, nodes, spaces, scale), out_...  79.3 us
    unnamed x1, local copies, waits for them, and re-layouts  4.86 us

profile of v2, /device:TPU:0, one launch (start us, length us, event | category | flops | bytes accessed | tf_op | source)
XLA Modules:
  0.0 85.7 jit_solution(10782160033543848031)
XLA Ops:
  0.0 0.8 broadcast_in_dim.2.kap_ref
  0.8 4.9 %copy.6 = bf16[128,2,8192]{2,0,1:T(8,128)(2,1)S(1)} copy(bf16[128,2,8192]{2,1,0:T(2,128)(2,1)} %param.2) | data formatting | bytes 8388608 | tf_op args[0]
  5.7 79.3 %gram_sums.1 = f32[128,64]{1,0:T(8,128)S(1)} custom-call(bf16[2,128,8192]{2,1,0:T(8,128)(2,1)S(1)} %bitcast.3, f32[2,8,8192]{2,1,0:T(8,128)S(1)} %broadcast_in_dim.2.kap_ref), custom_call_target="tpu_custom_call" | custom-call | tf_op jit(solution)/shard_map/gram_sums/pallas_call | solution.py:433
  85.0 0.7 copy.4

commit v3 on v2

--- a/solution.py
+++ b/solution.py
@@ -17,9 +17,9 @@
 
 def gram_kernel(
     nodes, spaces, scale, snap_ref, kap_ref, out_ref,
-    held, ends, ends_out, edge, side, kside, coef, image, gram, first, second, third, fourth,
+    held, ends, ends_out, edge, side, kside, coef, image, gram, first, second, third,
     own_sem, edge_sem, send_sem, recv_sem, esend, erecv, hsend, hrecv, ksend, krecv,
-    send1, recv1, send2, recv2, send3, recv3, send4, recv4,
+    send1, recv1, send2, recv2, send3, recv3,
 ):
     me = lax.axis_index("node")
     at = lax.axis_index("space")
@@ -29,7 +29,7 @@
     chunks = snap_rows // ROWS
     has_low = at > 0
     has_high = at < spaces - 1
-    summed = out_ref.shape[0] == snap_rows
+    summed = out_ref.shape[0] != nodes * snap_rows
     layers = spaces // 2 if summed else 1
 
     def edge_copy(index):
@@ -291,32 +291,28 @@
     apply(chunks - 1)
 
     order = nodes * snap_rows
-    half = snap_rows // 2
     core = lax.rem(at, 2)
     partner = at + 1 - 2 * core
     layer = at // 2
-    kept = pl.ds(pl.multiple_of(core * half, half), half)
-    given = pl.ds(pl.multiple_of((1 - core) * half, half), half)
-
-    def product(block):
-        def part(index, carry):
-            tile = jnp.zeros((snap_rows, 2 * snap_rows), jnp.float32)
-            for plane in range(2):
-                right = held[pl.ds(index * 2, 2), plane].reshape(2 * snap_rows, length)
-                tile = tile + lax.dot_general(
-                    image[block, plane], right, (((1,), (1,)), ((), ())),
-                    preferred_element_type=jnp.float32,
-                )
-            place = pl.ds(pl.multiple_of(index * 2 * snap_rows, 2 * snap_rows), 2 * snap_rows)
-            gram[block, :, place] = tile
-            return carry
-
-        lax.fori_loop(0, nodes // 2, part, 0)
+
+    def product(pair):
+        tile = jnp.zeros((order, 2 * snap_rows), jnp.float32)
+        for plane in range(2):
+            left = held[:, plane].reshape(order, length)
+            right = image[2 * pair : 2 * pair + 2, plane].reshape(2 * snap_rows, length)
+            tile = tile + lax.dot_general(
+                left, right, (((1,), (1,)), ((), ())), preferred_element_type=jnp.float32
+            )
+        for index in range(2):
+            part = tile[:, index * snap_rows : (index + 1) * snap_rows]
+            gram[2 * pair + index] = part.reshape(gram.shape[1:])
+
+    for pair in range(nodes // 2):
+        product(pair)
 
     def first_copy(turn):
-        block = lax.rem(me + turn, nodes)
-        return pltpu.make_async_remote_copy(
-            src_ref=gram.at[block, given],
+        return pltpu.make_async_remote_copy(
+            src_ref=gram.at[lax.rem(me + turn, nodes), :, 1 - core],
             dst_ref=first.at[turn],
             send_sem=send1.at[turn],
             recv_sem=recv1.at[turn],
@@ -335,9 +331,8 @@
         )
 
     def third_copy(turn):
-        dest = lax.rem(layer + turn, layers)
-        return pltpu.make_async_remote_copy(
-            src_ref=first.at[0, :, pl.ds(pl.multiple_of(dest * LANE, LANE), LANE)],
+        return pltpu.make_async_remote_copy(
+            src_ref=first.at[0, lax.rem(layer + turn, layers)],
             dst_ref=third.at[turn - 1],
             send_sem=send3.at[turn - 1],
             recv_sem=recv3.at[turn - 1],
@@ -345,50 +340,28 @@
             device_id_type=MESH,
         )
 
-    fourth_copy = pltpu.make_async_remote_copy(
-        src_ref=fourth.at[0],
-        dst_ref=fourth.at[1],
-        send_sem=send4,
-        recv_sem=recv4,
-        device_id={"space": partner},
-        device_id_type=MESH,
-    )
-
-    turns = list(range(1, nodes)) + [0]
-
-    def paired(turn):
-        first_copy(turn).wait_recv()
-        block = lax.rem(me + turn, nodes)
-        first[turn] = first[turn] + gram[block, kept]
-        if turn:
-            second_copy(turn).start()
-
     if summed:
-        for place, turn in enumerate(turns):
-            product(lax.rem(me + turn, nodes))
+        turns = list(range(1, nodes)) + [0]
+        for turn in turns:
             first_copy(turn).start()
-            if place:
-                paired(turns[place - 1])
-        paired(0)
+        for turn in turns:
+            first_copy(turn).wait_recv()
+            first[turn] = first[turn] + gram[lax.rem(me + turn, nodes), :, core]
+            if turn:
+                second_copy(turn).start()
         for turn in range(1, nodes):
             second_copy(turn).wait_recv()
-            first[0] = first[0] + second[turn - 1]
+        total = first[0]
+        for turn in range(1, nodes):
+            total = total + second[turn - 1]
+        first[0] = total
         for turn in range(1, layers):
             third_copy(turn).start()
-        own = first[0, :, pl.ds(pl.multiple_of(layer * LANE, LANE), LANE)]
+        own = first[0, layer]
         for turn in range(1, layers):
             third_copy(turn).wait_recv()
             own = own + third[turn - 1]
-        fourth[0] = own * scale
-        fourth_copy.start()
-        fourth_copy.wait()
-        width = LANE // 2
-
-        def taken(value):
-            return jnp.where(core == 0, value[:, :width], value[:, width:])
-
-        out_ref[kept] = taken(fourth[0])
-        out_ref[given] = taken(fourth[1])
+        out_ref[...] = own * scale
         for turn in range(nodes):
             first_copy(turn).wait_send()
         for turn in range(1, nodes):
@@ -397,8 +370,9 @@
             third_copy(turn).wait_send()
     else:
         for block in range(nodes):
-            product(block)
-            out_ref[block * snap_rows : (block + 1) * snap_rows] = gram[block]
+            out_ref[block * snap_rows : (block + 1) * snap_rows] = gram[block].reshape(
+                order, snap_rows
+            ).T
     for turn in range(1, nodes):
         ends_copy(turn).wait_send()
 
@@ -425,11 +399,12 @@
     length = width // nodes
     chunks = snap_rows // ROWS
     order = nodes * snap_rows
-    half = snap_rows // 2
     scale = 1.0 / math.sqrt(planes * spaces * NY * NZ)
-    summed = order // spaces == LANE // 2
+    share = order // spaces
+    summed = share % 8 == 0 and share * spaces == order and spaces % 2 == 0 and share >= 64
     layers = spaces // 2
-    shape = (snap_rows, order // spaces) if summed else (order, order)
+    shape = (share, snap_rows) if summed else (order, order)
+    blocks = (layers, 2, share) if summed else (1, 1, order)
     result = pl.pallas_call(
         functools.partial(gram_kernel, nodes, spaces, scale),
         out_shape=jax.ShapeDtypeStruct(shape, jnp.float32),
@@ -447,11 +422,10 @@
             pltpu.VMEM((2, 8, length), jnp.float32),
             pltpu.VMEM((11, 8, length), jnp.float32),
             pltpu.VMEM((nodes, planes, snap_rows, length), jnp.bfloat16),
-            pltpu.VMEM((nodes, snap_rows, order), jnp.float32),
-            pltpu.VMEM((nodes, half, order), jnp.float32),
-            pltpu.VMEM((nodes - 1, half, order), jnp.float32),
-            pltpu.VMEM((layers - 1, half, LANE), jnp.float32),
-            pltpu.VMEM((2, half, LANE), jnp.float32),
+            pltpu.VMEM((nodes,) + blocks + (snap_rows,), jnp.float32),
+            pltpu.VMEM((nodes, blocks[0], blocks[2], snap_rows), jnp.float32),
+            pltpu.VMEM((nodes - 1, blocks[0], blocks[2], snap_rows), jnp.float32),
+            pltpu.VMEM((layers - 1, blocks[2], snap_rows), jnp.float32),
             pltpu.SemaphoreType.DMA((chunks,)),
             pltpu.SemaphoreType.DMA((nodes - 1,)),
             pltpu.SemaphoreType.DMA((nodes - 1, chunks)),
@@ -468,8 +442,6 @@
             pltpu.SemaphoreType.DMA((nodes - 1,)),
             pltpu.SemaphoreType.DMA((layers - 1,)),
             pltpu.SemaphoreType.DMA((layers - 1,)),
-            pltpu.SemaphoreType.DMA,
-            pltpu.SemaphoreType.DMA,
         ],
         compiler_params=pltpu.CompilerParams(
             collective_id=0, has_side_effects=True, vmem_limit_bytes=48 * 1024 * 1024
@@ -480,7 +452,7 @@
         jnp.broadcast_to(kappa.astype(jnp.float32)[:, None], (planes, 8, width)),
     )
     if summed:
-        return result
+        return result.T
     mine = lax.psum_scatter(result, "node", scatter_dimension=0, tiled=True)
     return lax.psum_scatter(mine, "space", scatter_dimension=1, tiled=True) * scale
 

time: 85.9 us -> 83.9 us (0.977)
  Pallas kernels: 79.3 us -> 77.4 us
    pallas_call x1, Pallas kernels: 79.3 us -> 77.4 us  [per_device(): pl.pallas_call(functools.partial(gram_kernel, nodes, spaces, scale), out_...]
    unnamed x1 -> x2, local copies, waits for them, and re-layouts: 4.86 us -> 5.48 us
where the time goes in v3:
time: 83.9 us; the launch traced here: 83.7 us
  Pallas kernels  77.4 us (92%)
  local copies, waits for them, and re-layouts  6.27 us (7%)
    pallas_call x1, Pallas kernels, per_device(): pl.pallas_call(functools.partial(gram_kernel, nodes, spaces, scale), out_...  77.4 us
    unnamed x2, local copies, waits for them, and re-layouts  5.48 us

profile of v3, /device:TPU:0, one launch (start us, length us, event | category | flops | bytes accessed | tf_op | source)
XLA Modules:
  0.0 83.7 jit_solution(327382000877822429)
XLA Ops:
  0.0 0.8 broadcast_in_dim.2.kap_ref
  0.8 4.9 %copy.5 = bf16[128,2,8192]{2,0,1:T(8,128)(2,1)S(1)} copy(bf16[128,2,8192]{2,1,0:T(2,128)(2,1)} %param.2) | data formatting | bytes 8388608 | tf_op args[0]
  5.7 77.4 %gram_sums.1 = f32[64,128]{1,0:T(8,128)S(1)} custom-call(bf16[2,128,8192]{2,1,0:T(8,128)(2,1)S(1)} %bitcast.4, f32[2,8,8192]{2,1,0:T(8,128)S(1)} %broadcast_in_dim.2.kap_ref), custom_call_target="tpu_custom_call" | custom-call | tf_op jit(solution)/shard_map/gram_sums/pallas_call | solution.py:408
  83.0 0.6 copy.7

commit v4 on v3

--- a/solution.py
+++ b/solution.py
@@ -17,13 +17,13 @@
 
 def gram_kernel(
     nodes, spaces, scale, snap_ref, kap_ref, out_ref,
-    held, ends, ends_out, edge, side, kside, coef, image, gram, first, second, third,
-    own_sem, edge_sem, send_sem, recv_sem, esend, erecv, hsend, hrecv, ksend, krecv,
+    raw, sent, held, side, kside, coef, image, gram, first, second, third,
+    raw_sem, own_sem, send_sem, recv_sem, hsend, hrecv, ksend, krecv,
     send1, recv1, send2, recv2, send3, recv3,
 ):
     me = lax.axis_index("node")
     at = lax.axis_index("space")
-    snap_rows = snap_ref.shape[1]
+    snap_rows = snap_ref.shape[0]
     length = snap_ref.shape[2] // nodes
     tiles = length // LANE
     chunks = snap_rows // ROWS
@@ -32,16 +32,37 @@
     summed = out_ref.shape[0] != nodes * snap_rows
     layers = spaces // 2 if summed else 1
 
-    def edge_copy(index):
-        return pltpu.make_async_copy(
-            snap_ref.at[:, :, pl.ds((index + 1) * length - LANE, 2 * LANE)],
-            edge.at[index],
-            edge_sem.at[index],
-        )
-
-    for index in range(nodes - 1):
-        edge_copy(index).start()
-
+    def raw_copy(chunk):
+        rows = pl.ds(chunk * ROWS, ROWS)
+        return pltpu.make_async_copy(snap_ref.at[rows], raw.at[rows], raw_sem.at[chunk])
+
+    for chunk in range(chunks):
+        raw_copy(chunk).start()
+
+    low_rows = lax.broadcasted_iota(jnp.int32, (ROWS, LANE), 1) < NZ
+
+    def spread(chunk):
+        rows = pl.ds(pl.multiple_of(chunk * ROWS, ROWS), ROWS)
+        raw_copy(chunk).wait()
+        for plane in range(2):
+
+            def turned_tile(first):
+                value = raw[rows, plane, first : first + LANE].astype(jnp.float32)
+                return pltpu.roll(value, NZ, 1)
+
+            for dest in range(nodes):
+                low, high = (dest * length, (dest + 1) * length)
+                sent[dest, plane, rows, :length] = raw[rows, plane, low:high]
+                before = after = jnp.zeros((ROWS, LANE), jnp.float32)
+                if dest:
+                    before = turned_tile(low - LANE)
+                if dest < nodes - 1:
+                    after = turned_tile(high)
+                sent[dest, plane, rows, length:] = jnp.where(low_rows, before, after).astype(
+                    jnp.bfloat16
+                )
+
+    spread(0)
     barrier = pltpu.get_barrier_semaphore()
     for turn in range(1, nodes):
         pl.semaphore_signal(
@@ -86,7 +107,7 @@
     def own_copy(chunk):
         rows = pl.ds(chunk * ROWS, ROWS)
         return pltpu.make_async_copy(
-            snap_ref.at[:, rows, pl.ds(pl.multiple_of(me * length, LANE), length)],
+            sent.at[me, :, rows],
             held.at[me, :, rows],
             own_sem.at[chunk],
         )
@@ -95,7 +116,7 @@
         rows = pl.ds(chunk * ROWS, ROWS)
         peer = lax.rem(me + turn, nodes)
         return pltpu.make_async_remote_copy(
-            src_ref=snap_ref.at[:, rows, pl.ds(pl.multiple_of(peer * length, LANE), length)],
+            src_ref=sent.at[peer, :, rows],
             dst_ref=held.at[me, :, rows],
             send_sem=send_sem.at[turn - 1, chunk],
             recv_sem=recv_sem.at[turn - 1, chunk],
@@ -106,7 +127,7 @@
     def side_copy(chunk, high):
         rows = pl.ds(chunk * ROWS, ROWS)
         return pltpu.make_async_remote_copy(
-            src_ref=held.at[:, 1 if high else 0, rows],
+            src_ref=held.at[:, 1 if high else 0, rows, pl.ds(0, length)],
             dst_ref=side.at[0 if high else 1, :, rows],
             send_sem=hsend.at[0 if high else 1, chunk],
             recv_sem=hrecv.at[0 if high else 1, chunk],
@@ -124,17 +145,6 @@
             device_id_type=MESH,
         )
 
-    def ends_copy(turn):
-        peer = lax.rem(me + turn, nodes)
-        return pltpu.make_async_remote_copy(
-            src_ref=ends_out.at[peer],
-            dst_ref=ends.at[me],
-            send_sem=esend.at[turn - 1],
-            recv_sem=erecv.at[turn - 1],
-            device_id={"node": peer},
-            device_id_type=MESH,
-        )
-
     @pl.when(has_high)
     def _():
         kappa_copy(True).start()
@@ -150,22 +160,12 @@
         return carry
 
     begin(0, 0)
-    for index in range(nodes - 1):
-        edge_copy(index).wait()
-
-    wide_lower = lax.broadcasted_iota(jnp.int32, (snap_rows, LANE), 1) < NZ
-    for dest in range(nodes):
-        for plane in range(2):
-            before = after = jnp.zeros((snap_rows, LANE), jnp.float32)
-            if dest:
-                before = pltpu.roll(edge[dest - 1, plane, :, :LANE].astype(jnp.float32), NZ, 1)
-            if dest < nodes - 1:
-                after = pltpu.roll(edge[dest, plane, :, LANE:].astype(jnp.float32), NZ, 1)
-            ends_out[dest, plane] = jnp.where(wide_lower, before, after).astype(jnp.bfloat16)
-    for turn in range(1, nodes):
-        ends_copy(turn).start()
-    ends[me] = ends_out[me]
-    lax.fori_loop(1, chunks, begin, 0)
+
+    def follow(chunk, carry):
+        spread(chunk)
+        return begin(chunk, carry)
+
+    lax.fori_loop(1, chunks, follow, 0)
 
     @pl.when(has_high)
     def _():
@@ -247,7 +247,7 @@
             def load(plane, tile):
                 return wide(held[node, plane, rows, cols(tile)])
 
-            sides = [wide(ends[node, plane, rows, :]) for plane in range(2)]
+            sides = [load(plane, tiles) for plane in range(2)]
             now = [load(plane, 0) for plane in range(2)]
             turned = [pltpu.roll(v, NZ, 2) for v in now]
             last = list(sides)
@@ -279,8 +279,6 @@
         lax.fori_loop(0, nodes, one, 0)
 
     arrive(0)
-    for turn in range(1, nodes):
-        ends_copy(turn).wait_recv()
 
     def step(chunk, carry):
         arrive(chunk)
@@ -298,8 +296,8 @@
     def product(pair):
         tile = jnp.zeros((order, 2 * snap_rows), jnp.float32)
         for plane in range(2):
-            left = held[:, plane].reshape(order, length)
-            right = image[2 * pair : 2 * pair + 2, plane].reshape(2 * snap_rows, length)
+            left = held[:, plane, :, :length].reshape(order, length)
+            right = image[pl.ds(2 * pair, 2), plane].reshape(2 * snap_rows, length)
             tile = tile + lax.dot_general(
                 left, right, (((1,), (1,)), ((), ())), preferred_element_type=jnp.float32
             )
@@ -307,32 +305,30 @@
             part = tile[:, index * snap_rows : (index + 1) * snap_rows]
             gram[2 * pair + index] = part.reshape(gram.shape[1:])
 
-    for pair in range(nodes // 2):
-        product(pair)
-
-    def first_copy(turn):
-        return pltpu.make_async_remote_copy(
-            src_ref=gram.at[lax.rem(me + turn, nodes), :, 1 - core],
-            dst_ref=first.at[turn],
-            send_sem=send1.at[turn],
-            recv_sem=recv1.at[turn],
+    def first_copy(block):
+        return pltpu.make_async_remote_copy(
+            src_ref=gram.at[block, :, 1 - core],
+            dst_ref=first.at[block],
+            send_sem=send1.at[block],
+            recv_sem=recv1.at[block],
             device_id={"space": partner},
             device_id_type=MESH,
         )
 
     def second_copy(turn):
-        return pltpu.make_async_remote_copy(
-            src_ref=first.at[turn],
+        block = lax.rem(me + turn, nodes)
+        return pltpu.make_async_remote_copy(
+            src_ref=first.at[block],
             dst_ref=second.at[turn - 1],
             send_sem=send2.at[turn - 1],
             recv_sem=recv2.at[turn - 1],
-            device_id={"node": lax.rem(me + turn, nodes)},
+            device_id={"node": block},
             device_id_type=MESH,
         )
 
     def third_copy(turn):
         return pltpu.make_async_remote_copy(
-            src_ref=first.at[0, lax.rem(layer + turn, layers)],
+            src_ref=first.at[me, lax.rem(layer + turn, layers)],
             dst_ref=third.at[turn - 1],
             send_sem=send3.at[turn - 1],
             recv_sem=recv3.at[turn - 1],
@@ -341,23 +337,35 @@
         )
 
     if summed:
-        turns = list(range(1, nodes)) + [0]
-        for turn in turns:
-            first_copy(turn).start()
-        for turn in turns:
-            first_copy(turn).wait_recv()
-            first[turn] = first[turn] + gram[lax.rem(me + turn, nodes), :, core]
-            if turn:
-                second_copy(turn).start()
+        def joined(block):
+            first_copy(block).wait_recv()
+            first[block] = first[block] + gram[block, :, core]
+
+        away = nodes // 2 - 1 - me // 2
+        for index in range(nodes // 2):
+            pair = lax.rem(away + index, nodes // 2)
+            product(pair)
+            for place in range(2):
+                first_copy(2 * pair + place).start()
+            if index == 0:
+                ahead = pair
+        for place in range(2):
+            block = 2 * ahead + place
+            joined(block)
+            second_copy(lax.rem(block - me + nodes, nodes)).start()
+        block = me + 1 - 2 * lax.rem(me, 2)
+        joined(block)
+        second_copy(lax.rem(block - me + nodes, nodes)).start()
+        joined(me)
         for turn in range(1, nodes):
             second_copy(turn).wait_recv()
-        total = first[0]
+        total = first[me]
         for turn in range(1, nodes):
             total = total + second[turn - 1]
-        first[0] = total
+        first[me] = total
         for turn in range(1, layers):
             third_copy(turn).start()
-        own = first[0, layer]
+        own = first[me, layer]
         for turn in range(1, layers):
             third_copy(turn).wait_recv()
             own = own + third[turn - 1]
@@ -369,12 +377,12 @@
         for turn in range(1, layers):
             third_copy(turn).wait_send()
     else:
+        for pair in range(nodes // 2):
+            product(pair)
         for block in range(nodes):
             out_ref[block * snap_rows : (block + 1) * snap_rows] = gram[block].reshape(
                 order, snap_rows
             ).T
-    for turn in range(1, nodes):
-        ends_copy(turn).wait_send()
 
     def finish(chunk, carry):
         for turn in range(1, nodes):
@@ -414,10 +422,9 @@
         ],
         out_specs=pl.BlockSpec(memory_space=pltpu.VMEM),
         scratch_shapes=[
-            pltpu.VMEM((nodes, planes, snap_rows, length), jnp.bfloat16),
-            pltpu.VMEM((nodes, planes, snap_rows, LANE), jnp.bfloat16),
-            pltpu.VMEM((nodes, planes, snap_rows, LANE), jnp.bfloat16),
-            pltpu.VMEM((nodes - 1, planes, snap_rows, 2 * LANE), jnp.bfloat16),
+            pltpu.VMEM((snap_rows, planes, width), jnp.bfloat16),
+            pltpu.VMEM((nodes, planes, snap_rows, length + LANE), jnp.bfloat16),
+            pltpu.VMEM((nodes, planes, snap_rows, length + LANE), jnp.bfloat16),
             pltpu.VMEM((2, nodes, snap_rows, length), jnp.bfloat16),
             pltpu.VMEM((2, 8, length), jnp.float32),
             pltpu.VMEM((11, 8, length), jnp.float32),
@@ -427,11 +434,9 @@
             pltpu.VMEM((nodes - 1, blocks[0], blocks[2], snap_rows), jnp.float32),
             pltpu.VMEM((layers - 1, blocks[2], snap_rows), jnp.float32),
             pltpu.SemaphoreType.DMA((chunks,)),
-            pltpu.SemaphoreType.DMA((nodes - 1,)),
+            pltpu.SemaphoreType.DMA((chunks,)),
             pltpu.SemaphoreType.DMA((nodes - 1, chunks)),
             pltpu.SemaphoreType.DMA((nodes - 1, chunks)),
-            pltpu.SemaphoreType.DMA((nodes - 1,)),
-            pltpu.SemaphoreType.DMA((nodes - 1,)),
             pltpu.SemaphoreType.DMA((2, chunks)),
             pltpu.SemaphoreType.DMA((2, chunks)),
             pltpu.SemaphoreType.DMA((2,)),
@@ -444,11 +449,11 @@
             pltpu.SemaphoreType.DMA((layers - 1,)),
         ],
         compiler_params=pltpu.CompilerParams(
-            collective_id=0, has_side_effects=True, vmem_limit_bytes=48 * 1024 * 1024
+            collective_id=0, has_side_effects=True, vmem_limit_bytes=60 * 1024 * 1024
         ),
         name="gram_sums",
     )(
-        jnp.transpose(snapshots, (1, 0, 2)),
+        snapshots,
         jnp.broadcast_to(kappa.astype(jnp.float32)[:, None], (planes, 8, width)),
     )
     if summed:

time: 83.9 us -> 85.1 us (1.014)
  Pallas kernels: 77.4 us -> 81.9 us
  local copies, waits for them, and re-layouts: 6.27 us -> 2.96 us
    pallas_call x1, Pallas kernels: 77.4 us -> 81.9 us  [per_device(): pl.pallas_call(functools.partial(gram_kernel, nodes, spaces, scale), out_...]
    unnamed x2 -> x1, local copies, waits for them, and re-layouts: 5.48 us -> 1.38 us
where the time goes in v4:
time: 85.1 us; the launch traced here: 84.8 us
  Pallas kernels  81.9 us (96%)
  local copies, waits for them, and re-layouts  2.96 us (3%)
    pallas_call x1, Pallas kernels, per_device(): pl.pallas_call(functools.partial(gram_kernel, nodes, spaces, scale), out_...  81.9 us

profile of v4, /device:TPU:0, one launch (start us, length us, event | category | flops | bytes accessed | tf_op | source)
XLA Modules:
  0.0 84.8 jit_solution(7079183034090458575)
XLA Ops:
  0.0 1.6 %broadcast_in_dim.2.kap_ref = f32[2,8,8192]{2,1,0:T(8,128)} broadcast(bf16[2,8192]{1,0:T(2,128)(2,1)} %param.3), dimensions={0,2} | broadcast | bytes 557056 | tf_op jit(solution)/shard_map/broadcast_in_dim | solution.py:457
  1.6 81.9 %gram_sums.1 = f32[64,128]{1,0:T(8,128)} custom-call(bf16[128,2,8192]{2,1,0:T(2,128)(2,1)} %snap_ref.1, f32[2,8,8192]{2,1,0:T(8,128)} %broadcast_in_dim.2.kap_ref), custom_call_target="tpu_custom_call" | custom-call | tf_op jit(solution)/shard_map/gram_sums/pallas_call | solution.py:416
  83.5 1.4 %copy.4 = f32[128,64]{0,1:T(8,128)} copy(f32[128,64]{0,1:T(8,128)} %bitcast.1) | data formatting | bytes 65536

commit v5 on v4

--- a/solution.py
+++ b/solution.py
@@ -17,9 +17,9 @@
 
 def gram_kernel(
     nodes, spaces, scale, snap_ref, kap_ref, out_ref,
-    raw, sent, held, side, kside, coef, image, gram, first, second, third,
+    raw, sent, held, side, kown, kside, coef, image, gram, first, second, third, late, cross,
     raw_sem, own_sem, send_sem, recv_sem, hsend, hrecv, ksend, krecv,
-    send1, recv1, send2, recv2, send3, recv3,
+    send1, recv1, send2, recv2, send3, recv3, send4, recv4, send5, recv5,
 ):
     me = lax.axis_index("node")
     at = lax.axis_index("space")
@@ -63,6 +63,9 @@
                 )
 
     spread(0)
+    for plane in range(2):
+        values = kap_ref[plane : plane + 1, pl.ds(pl.multiple_of(me * length, LANE), length)]
+        kown[plane] = jnp.broadcast_to(values.astype(jnp.float32), (8, length))
     barrier = pltpu.get_barrier_semaphore()
     for turn in range(1, nodes):
         pl.semaphore_signal(
@@ -137,7 +140,7 @@
 
     def kappa_copy(high):
         return pltpu.make_async_remote_copy(
-            src_ref=kap_ref.at[1 if high else 0, :, pl.ds(pl.multiple_of(me * length, LANE), length)],
+            src_ref=kown.at[1 if high else 0],
             dst_ref=kside.at[0 if high else 1],
             send_sem=ksend.at[0 if high else 1],
             recv_sem=krecv.at[0 if high else 1],
@@ -186,18 +189,20 @@
     def cols(tile):
         return pl.ds(tile * LANE, LANE)
 
-    def mine(tile):
-        return pl.ds(pl.multiple_of((me * tiles + tile) * LANE, LANE), LANE)
-
     low_at = pl.ds(pl.multiple_of(jnp.maximum(me * tiles - 1, 0) * LANE, LANE), LANE)
     high_at = pl.ds(
         pl.multiple_of(jnp.minimum((me + 1) * tiles, nodes * tiles - 1) * LANE, LANE), LANE
     )
     for plane in range(2):
-        kap = [kap_ref[plane, :, mine(t)] for t in range(tiles)]
+
+        def beyond(place):
+            value = kap_ref[plane : plane + 1, place].astype(jnp.float32)
+            return pltpu.roll(jnp.broadcast_to(value, (8, LANE)), NZ, 1)
+
+        kap = [kown[plane, :, cols(t)] for t in range(tiles)]
         turned = [pltpu.roll(k, NZ, 1) for k in kap]
-        before = pltpu.roll(kap_ref[plane, :, low_at], NZ, 1)
-        after = pltpu.roll(kap_ref[plane, :, high_at], NZ, 1)
+        before = beyond(low_at)
+        after = beyond(high_at)
         before = before * jnp.where(me > 0, 1.0, 0.0)
         after = after * jnp.where(me < nodes - 1, 1.0, 0.0)
         for t in range(tiles):
@@ -209,7 +214,7 @@
             coef[4 * plane + 2, :, cols(t)] = 0.5 * (k + down)
             coef[4 * plane + 3, :, cols(t)] = rim * k
     for t in range(tiles):
-        low, high = (kap_ref[0, :, mine(t)], kap_ref[1, :, mine(t)])
+        low, high = (kown[0, :, cols(t)], kown[1, :, cols(t)])
         coef[8, :, cols(t)] = 0.5 * (low + kside[0, :, cols(t)])
         coef[9, :, cols(t)] = 0.5 * (low + high)
         coef[10, :, cols(t)] = 0.5 * (high + kside[1, :, cols(t)])
@@ -315,10 +320,14 @@
             device_id_type=MESH,
         )
 
+    share = gram.shape[3]
+    early = share * 5 // 8 // 8 * 8
+    one, two = (pl.ds(0, early), pl.ds(early, share - early))
+
     def second_copy(turn):
         block = lax.rem(me + turn, nodes)
         return pltpu.make_async_remote_copy(
-            src_ref=first.at[block],
+            src_ref=first.at[block, :, one],
             dst_ref=second.at[turn - 1],
             send_sem=send2.at[turn - 1],
             recv_sem=recv2.at[turn - 1],
@@ -328,11 +337,32 @@
 
     def third_copy(turn):
         return pltpu.make_async_remote_copy(
-            src_ref=first.at[me, lax.rem(layer + turn, layers)],
+            src_ref=first.at[me, lax.rem(layer + turn, layers), one],
             dst_ref=third.at[turn - 1],
             send_sem=send3.at[turn - 1],
             recv_sem=recv3.at[turn - 1],
             device_id={"space": lax.rem(at + 2 * turn, spaces)},
+            device_id_type=MESH,
+        )
+
+    def late_copy(turn):
+        return pltpu.make_async_remote_copy(
+            src_ref=first.at[:, lax.rem(layer + turn, layers), two],
+            dst_ref=late.at[turn - 1],
+            send_sem=send4.at[turn - 1],
+            recv_sem=recv4.at[turn - 1],
+            device_id={"space": lax.rem(at + 2 * turn, spaces)},
+            device_id_type=MESH,
+        )
+
+    def cross_copy(turn):
+        block = lax.rem(me + turn, nodes)
+        return pltpu.make_async_remote_copy(
+            src_ref=first.at[block, layer, two],
+            dst_ref=cross.at[turn - 1],
+            send_sem=send5.at[turn - 1],
+            recv_sem=recv5.at[turn - 1],
+            device_id={"node": block},
             device_id_type=MESH,
         )
 
@@ -357,19 +387,38 @@
         joined(block)
         second_copy(lax.rem(block - me + nodes, nodes)).start()
         joined(me)
+        for turn in range(1, layers):
+            late_copy(turn).start()
         for turn in range(1, nodes):
             second_copy(turn).wait_recv()
-        total = first[me]
+        total = first[me, :, one]
         for turn in range(1, nodes):
             total = total + second[turn - 1]
-        first[me] = total
+        first[me, :, one] = total
         for turn in range(1, layers):
             third_copy(turn).start()
-        own = first[me, layer]
+        for turn in range(1, layers):
+            late_copy(turn).wait_recv()
+        total = first[:, layer, two]
+        for turn in range(1, layers):
+            total = total + late[turn - 1]
+        first[:, layer, two] = total
+        for turn in range(1, nodes):
+            cross_copy(turn).start()
+        own = first[me, layer, one]
         for turn in range(1, layers):
             third_copy(turn).wait_recv()
             own = own + third[turn - 1]
-        out_ref[...] = own * scale
+        out_ref[one] = own * scale
+        own = first[me, layer, two]
+        for turn in range(1, nodes):
+            cross_copy(turn).wait_recv()
+            own = own + cross[turn - 1]
+        out_ref[two] = own * scale
+        for turn in range(1, nodes):
+            cross_copy(turn).wait_send()
+        for turn in range(1, layers):
+            late_copy(turn).wait_send()
         for turn in range(nodes):
             first_copy(turn).wait_send()
         for turn in range(1, nodes):
@@ -412,6 +461,7 @@
     summed = share % 8 == 0 and share * spaces == order and spaces % 2 == 0 and share >= 64
     layers = spaces // 2
     shape = (share, snap_rows) if summed else (order, order)
+    early = share * 5 // 8 // 8 * 8 if summed else 8
     blocks = (layers, 2, share) if summed else (1, 1, order)
     result = pl.pallas_call(
         functools.partial(gram_kernel, nodes, spaces, scale),
@@ -427,12 +477,15 @@
             pltpu.VMEM((nodes, planes, snap_rows, length + LANE), jnp.bfloat16),
             pltpu.VMEM((2, nodes, snap_rows, length), jnp.bfloat16),
             pltpu.VMEM((2, 8, length), jnp.float32),
+            pltpu.VMEM((2, 8, length), jnp.float32),
             pltpu.VMEM((11, 8, length), jnp.float32),
             pltpu.VMEM((nodes, planes, snap_rows, length), jnp.bfloat16),
             pltpu.VMEM((nodes,) + blocks + (snap_rows,), jnp.float32),
             pltpu.VMEM((nodes, blocks[0], blocks[2], snap_rows), jnp.float32),
-            pltpu.VMEM((nodes - 1, blocks[0], blocks[2], snap_rows), jnp.float32),
-            pltpu.VMEM((layers - 1, blocks[2], snap_rows), jnp.float32),
+            pltpu.VMEM((nodes - 1, blocks[0], early, snap_rows), jnp.float32),
+            pltpu.VMEM((layers - 1, early, snap_rows), jnp.float32),
+            pltpu.VMEM((layers - 1, nodes, blocks[2] - early, snap_rows), jnp.float32),
+            pltpu.VMEM((nodes - 1, blocks[2] - early, snap_rows), jnp.float32),
             pltpu.SemaphoreType.DMA((chunks,)),
             pltpu.SemaphoreType.DMA((chunks,)),
             pltpu.SemaphoreType.DMA((nodes - 1, chunks)),
@@ -447,14 +500,18 @@
             pltpu.SemaphoreType.DMA((nodes - 1,)),
             pltpu.SemaphoreType.DMA((layers - 1,)),
             pltpu.SemaphoreType.DMA((layers - 1,)),
+            pltpu.SemaphoreType.DMA((layers - 1,)),
+            pltpu.SemaphoreType.DMA((layers - 1,)),
+            pltpu.SemaphoreType.DMA((nodes - 1,)),
+            pltpu.SemaphoreType.DMA((nodes - 1,)),
         ],
         compiler_params=pltpu.CompilerParams(
-            collective_id=0, has_side_effects=True, vmem_limit_bytes=60 * 1024 * 1024
+            collective_id=0, has_side_effects=True, vmem_limit_bytes=55 * 1024 * 1024
         ),
         name="gram_sums",
     )(
         snapshots,
-        jnp.broadcast_to(kappa.astype(jnp.float32)[:, None], (planes, 8, width)),
+        kappa,
     )
     if summed:
         return result.T

time: 85.1 us -> 81.5 us (0.958)
  Pallas kernels: 81.9 us -> 79.9 us
  local copies, waits for them, and re-layouts: 2.96 us -> 1.38 us
    pallas_call x1, Pallas kernels: 81.9 us -> 79.9 us  [per_device(): pl.pallas_call(functools.partial(gram_kernel, nodes, spaces, scale), out_...]
    broadcast_in_dim x1 -> x0, local copies, waits for them, and re-layouts: 1.58 us -> none  [per_device(): jnp.broadcast_to(kappa.astype(jnp.float32)[:, None], (planes, 8, width))]
where the time goes in v5:
time: 81.5 us; the launch traced here: 81.3 us
  Pallas kernels  79.9 us (98%)
  local copies, waits for them, and re-layouts  1.38 us (2%)
    pallas_call x1, Pallas kernels, per_device(): pl.pallas_call(functools.partial(gram_kernel, nodes, spaces, scale), out_...  79.9 us

profile of v5, /device:TPU:0, one launch (start us, length us, event | category | flops | bytes accessed | tf_op | source)
XLA Modules:
  0.0 81.3 jit_solution(14458233632775633963)
XLA Ops:
  0.0 79.9 %gram_sums.1 = f32[64,128]{1,0:T(8,128)} custom-call(bf16[128,2,8192]{2,1,0:T(2,128)(2,1)} %snap_ref.1, bf16[2,8192]{1,0:T(2,128)(2,1)} %kap_ref.1), custom_call_target="tpu_custom_call" | custom-call | tf_op jit(solution)/shard_map/gram_sums/pallas_call | solution.py:466
  79.9 1.4 %copy.4 = f32[128,64]{0,1:T(8,128)} copy(f32[128,64]{0,1:T(8,128)} %bitcast.1) | data formatting | bytes 65536

commit v6 on v5

--- a/solution.py
+++ b/solution.py
@@ -232,7 +232,7 @@
         def _():
             side_copy(chunk, False).start()
 
-    lower3 = lax.broadcasted_iota(jnp.int32, (ROWS // 8, 8, LANE), 2) < NZ
+    lower3 = lax.broadcasted_iota(jnp.int32, (ROWS // 4, 8, LANE), 2) < NZ
 
     def apply(chunk):
         @pl.when(has_high)
@@ -245,9 +245,12 @@
 
         rows = pl.ds(chunk * ROWS, ROWS)
 
-        def one(node, carry):
+        def one(index, carry):
+            node = pl.ds(2 * index, 2)
+            ready = []
+
             def wide(value):
-                return value.astype(jnp.float32).reshape(ROWS // 8, 8, LANE)
+                return value.astype(jnp.float32).reshape(ROWS // 4, 8, LANE)
 
             def load(plane, tile):
                 return wide(held[node, plane, rows, cols(tile)])
@@ -275,13 +278,16 @@
                     total = total + coef[4 * plane + 2, :, cols(t)] * (v - down)
                     total = total + coef[8 + 2 * plane, :, cols(t)] * (v - beside[plane])
                     total = total - mid if plane else total + mid
-                    image[node, plane, rows, cols(t)] = total.reshape(ROWS, LANE).astype(
-                        jnp.bfloat16
-                    )
+                    ready.append(total.reshape(2, ROWS, LANE).astype(jnp.bfloat16))
+                if t:
+                    for plane in range(2):
+                        image[node, plane, rows, cols(t - 1)] = ready.pop(0)
                 last, turned, now = (turned, coming, later)
+            for plane in range(2):
+                image[node, plane, rows, cols(tiles - 1)] = ready.pop(0)
             return carry
 
-        lax.fori_loop(0, nodes, one, 0)
+        lax.fori_loop(0, nodes // 2, one, 0)
 
     arrive(0)
 
@@ -506,7 +512,7 @@
             pltpu.SemaphoreType.DMA((nodes - 1,)),
         ],
         compiler_params=pltpu.CompilerParams(
-            collective_id=0, has_side_effects=True, vmem_limit_bytes=55 * 1024 * 1024
+            collective_id=0, has_side_effects=True, vmem_limit_bytes=52 * 1024 * 1024
         ),
         name="gram_sums",
     )(

time: 81.5 us -> 82.2 us (level)
  no operation moved by 1% of the time
where the time goes in v6:
time: 82.2 us; the launch traced here: 82 us
  Pallas kernels  80.6 us (98%)
  local copies, waits for them, and re-layouts  1.37 us (2%)
    pallas_call x1, Pallas kernels, per_device(): pl.pallas_call(functools.partial(gram_kernel, nodes, spaces, scale), out_...  80.6 us

profile of v6, /device:TPU:0, one launch (start us, length us, event | category | flops | bytes accessed | tf_op | source)
XLA Modules:
  0.0 82.0 jit_solution(15762158650450695886)
XLA Ops:
  0.0 0.0 copy-start
  0.0 0.8 copy-done
  0.8 80.6 %gram_sums.1 = f32[64,128]{1,0:T(8,128)S(1)} custom-call(bf16[128,2,8192]{2,1,0:T(2,128)(2,1)} %snap_ref.1, bf16[2,8192]{1,0:T(2,128)(2,1)S(1)} %copy-done), custom_call_target="tpu_custom_call" | custom-call | tf_op jit(solution)/shard_map/gram_sums/pallas_call | solution.py:472
  81.4 0.6 copy.4
Async XLA Ops:
  0.0 0.8 copy-start

commit v7 on v5

--- a/solution.py
+++ b/solution.py
@@ -36,8 +36,7 @@
         rows = pl.ds(chunk * ROWS, ROWS)
         return pltpu.make_async_copy(snap_ref.at[rows], raw.at[rows], raw_sem.at[chunk])
 
-    for chunk in range(chunks):
-        raw_copy(chunk).start()
+    raw_copy(0).start()
 
     low_rows = lax.broadcasted_iota(jnp.int32, (ROWS, LANE), 1) < NZ
 
@@ -63,6 +62,8 @@
                 )
 
     spread(0)
+    for chunk in range(1, chunks):
+        raw_copy(chunk).start()
     for plane in range(2):
         values = kap_ref[plane : plane + 1, pl.ds(pl.multiple_of(me * length, LANE), length)]
         kown[plane] = jnp.broadcast_to(values.astype(jnp.float32), (8, length))

time: 81.5 us -> 81.6 us (level)
  no operation moved by 1% of the time
where the time goes in v7:
time: 81.6 us; the launch traced here: 81.3 us
  Pallas kernels  79.9 us (98%)
  local copies, waits for them, and re-layouts  1.38 us (2%)
    pallas_call x1, Pallas kernels, per_device(): pl.pallas_call(functools.partial(gram_kernel, nodes, spaces, scale), out_...  79.9 us

profile of v7, /device:TPU:0, one launch (start us, length us, event | category | flops | bytes accessed | tf_op | source)
XLA Modules:
  0.0 81.3 jit_solution(5490749872114871057)
XLA Ops:
  0.0 79.9 %gram_sums.1 = f32[64,128]{1,0:T(8,128)} custom-call(bf16[128,2,8192]{2,1,0:T(2,128)(2,1)} %snap_ref.1, bf16[2,8192]{1,0:T(2,128)(2,1)} %kap_ref.1), custom_call_target="tpu_custom_call" | custom-call | tf_op jit(solution)/shard_map/gram_sums/pallas_call | solution.py:467
  79.9 1.4 %copy.4 = f32[128,64]{0,1:T(8,128)} copy(f32[128,64]{0,1:T(8,128)} %bitcast.1) | data formatting | bytes 65536
